TPU v7x, 1024 devices: a whole 4x4x32 slice. The times are simulated.
1024 devices in a mesh: dp: 32 (over z), node: 8 (over y, core), local: 4 (over x).
Axes of the slice: x: 4, y: 4, z: 32, core: 2. Of those that a mesh axis runs over, the one named last changes fastest.
Arguments:
- tokens: bfloat16 [1024, 7168], P(('dp', 'local')), may hold values from -6 to 6
- out_grad: bfloat16 [1024, 7168], P(('dp', 'local')), may hold values from -1.1953125 to 1.1953125
- picks: int32 [1024, 8], P(('dp', 'local')), may hold values from 0 to 31, all different within a row; in each aligned block of 8 rows (0 to 7, 8 to 15, ...) at most 4 rows name the same one
- gates: bfloat16 [1024, 8], P(('dp', 'local')), may hold values from 0.099609375 to 1
- w_gate: bfloat16 [32, 7168, 1024], P('dp', None, 'node'), may hold values from -0.0625 to 0.0625
- w_up: bfloat16 [32, 7168, 1024], P('dp', None, 'node'), may hold values from -0.0625 to 0.0625
- w_down: bfloat16 [32, 1024, 7168], P('dp', 'node'), may hold values from -0.1875 to 0.1875
Outputs:
- in_grad: bfloat16 [1024, 7168], P(('dp', 'local'), 'node')
- gate_grad: float32 [1024, 8], P(('dp', 'local'))
- grad_gate_w: bfloat16 [32, 7168, 1024], P('dp', 'local', 'node')
- grad_up_w: bfloat16 [32, 7168, 1024], P('dp', 'local', 'node')
- grad_down_w: bfloat16 [32, 1024, 7168], P('dp', 'node', 'local')
Inputs may be any that keep to these rules, and one draw needn't show every extreme that they name: Each row names 8 different experts. Among the picks of one device's 8 tokens no expert is named more than 4 times; some expert is named exactly 4 times.
All inputs are finite; a program needn't handle non-finite values.
Results may differ from a plain program's by a relative error of at most 0.0059.
Values may be sent and summed in bfloat16 or wider, within the bound.
A program may use at most 64 MiB of HBM per device.

v0:
```python
import jax
import jax.numpy as jnp
from jax import lax
from jax.sharding import PartitionSpec as P


def contract_first(left, right):
    return lax.dot_general(
        left, right, (((0,), (0,)), ((), ())), preferred_element_type=jnp.float32
    )


def contract_last(left, right):
    return lax.dot_general(
        left, right, (((1,), (1,)), ((), ())), preferred_element_type=jnp.float32
    )


def body(tokens, out_grad, picks, gates, w_gate, w_up, w_down):
    tok_dev = tokens.shape[0]
    width = tokens.shape[1]
    top_count = picks.shape[1]
    expert_count = lax.axis_size("dp")
    node_count = lax.axis_size("node")
    local_count = lax.axis_size("local")
    capacity = max(2, 2 * tok_dev * top_count // expert_count)
    slot_rows = expert_count * capacity
    pick_count = tok_dev * top_count
    share = width // node_count
    flat_picks = picks.reshape(pick_count)
    position = jnp.arange(pick_count, dtype=jnp.int32)
    matching = flat_picks[:, None] == flat_picks[None, :]
    earlier = position[None, :] < position[:, None]
    rank_in = jnp.sum(jnp.logical_and(matching, earlier), axis=1)
    slot_of = flat_picks * capacity + rank_in
    slot_ids = jnp.arange(slot_rows, dtype=jnp.int32)
    pick_table = (slot_of[None, :] == slot_ids[:, None]).astype(jnp.float32)
    token_table = jnp.sum(pick_table.reshape(slot_rows, tok_dev, top_count), axis=2)
    token_table_b = token_table.astype(jnp.bfloat16)
    send_gate = jnp.dot(
        pick_table.astype(jnp.bfloat16),
        gates.reshape(pick_count, 1),
        preferred_element_type=jnp.float32,
    ).astype(jnp.bfloat16)
    send_x = jnp.dot(token_table_b, tokens, preferred_element_type=jnp.float32).astype(jnp.bfloat16)
    send_dy = jnp.dot(token_table_b, out_grad, preferred_element_type=jnp.float32).astype(
        jnp.bfloat16
    )
    arrived_x, arrived_dy, arrived_gate = (
        lax.all_to_all(
            send_x.reshape(expert_count, capacity, width),
            "dp",
            split_axis=0,
            concat_axis=0,
            tiled=True,
        ),
        lax.all_to_all(
            send_dy.reshape(expert_count, capacity, width),
            "dp",
            split_axis=0,
            concat_axis=0,
            tiled=True,
        ),
        lax.all_to_all(
            send_gate.reshape(expert_count, capacity), "dp", split_axis=0, concat_axis=0, tiled=True
        ),
    )
    arrived_x = arrived_x.reshape(slot_rows, width)
    arrived_dy = arrived_dy.reshape(slot_rows, width)
    gate_col = arrived_gate.reshape(slot_rows, 1).astype(jnp.float32)
    gate_mat = w_gate[0]
    up_mat = w_up[0]
    down_mat = w_down[0]
    hidden = gate_mat.shape[1]
    gate_pre = jnp.dot(arrived_x, gate_mat, preferred_element_type=jnp.float32)
    up_pre = jnp.dot(arrived_x, up_mat, preferred_element_type=jnp.float32)
    sigmoid_pre = jax.nn.sigmoid(gate_pre)
    act = gate_pre * sigmoid_pre * up_pre
    act_b = act.astype(jnp.bfloat16)
    back = contract_last(arrived_dy, down_mat)
    gate_part = jnp.sum(back * act, axis=1)
    scaled = (gate_col * arrived_dy.astype(jnp.float32)).astype(jnp.bfloat16)
    d_act = gate_col * back
    d_up = (d_act * gate_pre * sigmoid_pre).astype(jnp.bfloat16)
    d_pre = (d_act * up_pre * sigmoid_pre * (1.0 + gate_pre * (1.0 - sigmoid_pre))).astype(
        jnp.bfloat16
    )
    slot_grad = contract_last(d_pre, gate_mat) + contract_last(d_up, up_mat)
    column_width = width // local_count
    spread = (slot_rows, local_count, hidden)
    got = (
        lax.all_to_all(
            arrived_x.reshape(slot_rows, local_count, column_width),
            "local",
            split_axis=1,
            concat_axis=0,
            tiled=True,
        ),
        lax.all_to_all(
            scaled.reshape(slot_rows, local_count, column_width),
            "local",
            split_axis=1,
            concat_axis=0,
            tiled=True,
        ),
        lax.all_to_all(
            jnp.broadcast_to(act_b[:, None, :], spread),
            "local",
            split_axis=1,
            concat_axis=0,
            tiled=True,
        ),
        lax.all_to_all(
            jnp.broadcast_to(d_up[:, None, :], spread),
            "local",
            split_axis=1,
            concat_axis=0,
            tiled=True,
        ),
        lax.all_to_all(
            jnp.broadcast_to(d_pre[:, None, :], spread),
            "local",
            split_axis=1,
            concat_axis=0,
            tiled=True,
        ),
    )
    column_x = got[0].reshape(-1, column_width)
    column_scaled = got[1].reshape(-1, column_width)
    all_act = got[2].reshape(-1, hidden)
    all_up = got[3].reshape(-1, hidden)
    all_pre = got[4].reshape(-1, hidden)
    grad_gate_w = contract_first(column_x, all_pre).astype(jnp.bfloat16)[None]
    grad_up_w = contract_first(column_x, all_up).astype(jnp.bfloat16)[None]
    grad_down_w = contract_first(all_act, column_scaled).astype(jnp.bfloat16)[None]
    summed_grad, summed_gate = (
        lax.psum_scatter(
            slot_grad.reshape(expert_count, capacity, node_count, share),
            "node",
            scatter_dimension=2,
            tiled=True,
        ),
        lax.psum_scatter(
            jnp.broadcast_to(
                gate_part.reshape(expert_count, capacity, 1, 1),
                (expert_count, capacity, node_count, 1),
            ),
            "node",
            scatter_dimension=2,
            tiled=True,
        ),
    )
    back_grad, back_gate = (
        lax.all_to_all(
            summed_grad.reshape(expert_count, capacity, share),
            "dp",
            split_axis=0,
            concat_axis=0,
            tiled=True,
        ),
        lax.all_to_all(
            summed_gate.reshape(expert_count, capacity),
            "dp",
            split_axis=0,
            concat_axis=0,
            tiled=True,
        ),
    )
    in_grad = jnp.sum(
        back_grad.reshape(slot_rows, share)[slot_of].reshape(tok_dev, top_count, share), axis=1
    )
    gate_grad = back_gate.reshape(slot_rows)[slot_of].reshape(tok_dev, top_count)
    return (in_grad.astype(jnp.bfloat16), gate_grad, grad_gate_w, grad_up_w, grad_down_w)


def solution(mesh):
    placed = (
        P(("dp", "local"), None),
        P(("dp", "local"), None),
        P(("dp", "local"), None),
        P(("dp", "local"), None),
        P("dp", None, "node"),
        P("dp", None, "node"),
        P("dp", "node", None),
    )
    return jax.shard_map(
        body,
        mesh=mesh,
        in_specs=placed,
        out_specs=(
            P(("dp", "local"), "node"),
            P(("dp", "local"), None),
            P("dp", "local", "node"),
            P("dp", "local", "node"),
            P("dp", "node", "local"),
        ),
        check_vma=False,
    )
```

profile of v0, /device:TPU:24, one launch (start us, length us, event | category | flops | bytes accessed | tf_op | source)
XLA Modules:
  0.0 637.5 jit_solution(18020849770139042607)
XLA Ops:
  9.9 28.7 %all-to-all-start = ((bf16[32,1,4]{2,1,0:T(2,128)(2,1)}), bf16[32,1,4]{2,1,0:T(2,128)(2,1)S(1)}, u32[]{:S(2)}, u32[]{:S(2)}) async-start(bf16[32,1,4]{2,1,0:T(2,128)(2,1)} %all_to_all.98), calls=%async_computation | async-start | bytes 32768 | tf_op jit(solution)/shard_map/all_to_all | solution.py:64
  39.5 2.8 convolution_convert_fusion
  42.3 4.1 reshape.165
  46.4 14.5 %all-to-all-done = bf16[32,1,4]{2,1,0:T(2,128)(2,1)S(1)} async-done(((bf16[32,1,4]{2,1,0:T(2,128)(2,1)}), bf16[32,1,4]{2,1,0:T(2,128)(2,1)S(1)}, u32[]{:S(2)}, u32[]{:S(2)}) %all-to-all-start) | async-done | bytes 288 | tf_op jit(solution)/shard_map/all_to_all | solution.py:64
  61.0 7.5 %all-to-all-start.2 = ((bf16[32,4,7168]{2,1,0:T(4,128)(2,1)}), bf16[32,4,7168]{2,1,0:T(4,128)(2,1)}, u32[]{:S(2)}, u32[]{:S(2)}) async-start(bf16[32,4,7168]{2,1,0:T(4,128)(2,1)} %reshape.165), calls=%async_computation.2 | async-start | bytes 3670016 | tf_op jit(solution)/shard_map/all_to_all | solution.py:50
  70.4 4.1 reshape.163
  74.5 163.5 %all-to-all-done.2 = bf16[32,4,7168]{2,1,0:T(4,128)(2,1)} async-done(((bf16[32,4,7168]{2,1,0:T(4,128)(2,1)}), bf16[32,4,7168]{2,1,0:T(4,128)(2,1)}, u32[]{:S(2)}, u32[]{:S(2)}) %all-to-all-start.2) | async-done | bytes 1835040 | tf_op jit(solution)/shard_map/all_to_all | solution.py:50
  238.0 10.0 %all-to-all-start.1 = ((bf16[32,4,7168]{2,1,0:T(4,128)(2,1)}), bf16[32,4,7168]{2,1,0:T(4,128)(2,1)}, u32[]{:S(2)}, u32[]{:S(2)}) async-start(bf16[32,4,7168]{2,1,0:T(4,128)(2,1)} %reshape.163), calls=%async_computation.1 | async-start | bytes 3670016 | tf_op jit(solution)/shard_map/all_to_all | solution.py:57
  248.2 4.0 reshape.166
  255.6 162.1 %all-to-all-done.1 = bf16[32,4,7168]{2,1,0:T(4,128)(2,1)} async-done(((bf16[32,4,7168]{2,1,0:T(4,128)(2,1)}), bf16[32,4,7168]{2,1,0:T(4,128)(2,1)}, u32[]{:S(2)}, u32[]{:S(2)}) %all-to-all-start.1) | async-done | bytes 1835040 | tf_op jit(solution)/shard_map/all_to_all | solution.py:57
  417.6 3.9 reshape.164
  421.6 2.7 multiply_reduce_fusion
  427.1 3.9 copy.42
  432.5 21.7 %all-reduce = f32[32,4,8,1]{0,1,3,2:T(4,128)S(1)} all-reduce(f32[32,4,8,1]{0,1,3,2:T(4,128)S(1)} %broadcast_in_dim.17), channel_id=3, replica_groups=mesh['dp'=32,'node'=8,'local'=4] {'node'}, use_global_device_ids=true, to_apply=%region_5.0.clone | all-reduce | flops 1024 | bytes 8192
  455.6 10.7 %all-to-all-start.4 = ((f32[32,1,4]{2,1,0:T(1,128)}), f32[32,1,4]{2,1,0:T(1,128)S(1)}, u32[]{:S(2)}, u32[]{:S(2)}) async-start(f32[32,1,4]{2,1,0:T(1,128)} %copy.45), calls=%async_computation.5 | async-start | bytes 32768 | tf_op jit(solution)/shard_map/all_to_all | solution.py:161
  466.5 22.5 %all-to-all-done.4 = f32[32,1,4]{2,1,0:T(1,128)S(1)} async-done(((f32[32,1,4]{2,1,0:T(1,128)}), f32[32,1,4]{2,1,0:T(1,128)S(1)}, u32[]{:S(2)}, u32[]{:S(2)}) %all-to-all-start.4) | async-done | bytes 544 | tf_op jit(solution)/shard_map/all_to_all | solution.py:161
  489.7 4.3 all-to-all-start.7
  494.0 5.9 all-to-all-done.7
  499.9 8.4 %all_to_all.109 = bf16[128,4,128]{2,0,1:T(8,128)(2,1)S(1)} all-to-all(bf16[128,4,128]{2,0,1:T(8,128)(2,1)S(1)} %broadcast_in_dim.18), channel_id=1, replica_groups=mesh['dp'=32,'node'=8,'local'=4] {'local'}, dimensions={1} | all-to-all | bytes 262144 | tf_op jit(solution)/shard_map/all_to_all | solution.py:120
  509.0 3.3 all-to-all-start.8
  512.3 4.6 reshape_reshape.3
  516.9 4.4 copy.46
  521.3 4.8 all-to-all-start.5
  526.0 4.9 reshape.179
  531.0 4.1 fusion
  535.0 11.7 %all-to-all-done.5 = bf16[128,4,1792]{0,2,1:T(8,128)(2,1)} async-done(((bf16[128,4,1792]{0,2,1:T(8,128)(2,1)}), bf16[128,4,1792]{0,2,1:T(8,128)(2,1)}, u32[]{:S(2)}, u32[]{:S(2)}) %all-to-all-start.5) | async-done | bytes 1835040 | tf_op jit(solution)/shard_map/all_to_all | solution.py:92
  546.7 4.4 all-to-all-start.9
  553.2 17.5 %all-to-all-done.9 = bf16[128,4,1792]{2,0,1:T(8,128)(2,1)} async-done(((bf16[128,4,1792]{2,0,1:T(8,128)(2,1)}), bf16[128,4,1792]{2,0,1:T(8,128)(2,1)}, u32[]{:S(2)}, u32[]{:S(2)}) %all-to-all-start.9) | async-done | bytes 1835040 | tf_op jit(solution)/shard_map/all_to_all | solution.py:99
  570.8 3.9 all-to-all-start.3
  580.2 2.9 fusion.6
  583.1 2.9 fusion.5
  586.1 43.1 %all-to-all-done.3 = f32[32,4,896]{2,1,0:T(4,128)S(1)} async-done(((f32[32,4,896]{2,1,0:T(4,128)}), f32[32,4,896]{2,1,0:T(4,128)S(1)}, u32[]{:S(2)}, u32[]{:S(2)}) %all-to-all-start.3) | async-done | bytes 458784 | tf_op jit(solution)/shard_map/all_to_all | solution.py:154
  (55 shorter events, 25.6 us)
Async XLA Ops:
  7.2 245.0 %copy-start = (bf16[1,7168,128]{2,1,0:T(8,128)(2,1)S(1)}, bf16[1,7168,128]{2,1,0:T(8,128)(2,1)}, u32[]{:S(2)}) copy-start(bf16[1,7168,128]{2,1,0:T(8,128)(2,1)} %param.11) | copy-start | bytes 5505028
  9.9 51.1 %all-to-all-start = ((bf16[32,1,4]{2,1,0:T(2,128)(2,1)}), bf16[32,1,4]{2,1,0:T(2,128)(2,1)S(1)}, u32[]{:S(2)}, u32[]{:S(2)}) async-start(bf16[32,1,4]{2,1,0:T(2,128)(2,1)} %all_to_all.98), calls=%async_computation | async-start | bytes 32768 | tf_op jit(solution)/shard_map/all_to_all | solution.py:64
  46.4 22.1 %copy-start.4 = (bf16[8,7168]{1,0:T(8,128)(2,1)S(1)}, bf16[8,7168]{1,0:T(8,128)(2,1)}, u32[]{:S(2)}) copy-start(bf16[8,7168]{1,0:T(8,128)(2,1)} %param.8) | copy-start | bytes 344068
  61.0 177.0 %all-to-all-start.2 = ((bf16[32,4,7168]{2,1,0:T(4,128)(2,1)}), bf16[32,4,7168]{2,1,0:T(4,128)(2,1)}, u32[]{:S(2)}, u32[]{:S(2)}) async-start(bf16[32,4,7168]{2,1,0:T(4,128)(2,1)} %reshape.165), calls=%async_computation.2 | async-start | bytes 3670016 | tf_op jit(solution)/shard_map/all_to_all | solution.py:50
  238.0 179.7 %all-to-all-start.1 = ((bf16[32,4,7168]{2,1,0:T(4,128)(2,1)}), bf16[32,4,7168]{2,1,0:T(4,128)(2,1)}, u32[]{:S(2)}, u32[]{:S(2)}) async-start(bf16[32,4,7168]{2,1,0:T(4,128)(2,1)} %reshape.163), calls=%async_computation.1 | async-start | bytes 3670016 | tf_op jit(solution)/shard_map/all_to_all | solution.py:57
  248.0 303.2 %reduce-scatter.2.cloned.1.call-start = ((), (), s32[]{:S(2)}) async-start(), calls=%async_computation.11 | async-start | bytes 4128768 | tf_op jit(solution)/shard_map/reduce_scatter | solution.py:137
  252.1 2.5 copy-start.1
  252.1 2.6 copy-start.2
  424.3 1.5 copy-start.3
  455.6 33.4 %all-to-all-start.4 = ((f32[32,1,4]{2,1,0:T(1,128)}), f32[32,1,4]{2,1,0:T(1,128)S(1)}, u32[]{:S(2)}, u32[]{:S(2)}) async-start(f32[32,1,4]{2,1,0:T(1,128)} %copy.45), calls=%async_computation.5 | async-start | bytes 32768 | tf_op jit(solution)/shard_map/all_to_all | solution.py:161
  489.7 10.2 %all-to-all-start.7 = ((bf16[128,4,128]{2,0,1:T(8,128)(2,1)}), bf16[128,4,128]{2,0,1:T(8,128)(2,1)S(1)}, u32[]{:S(2)}, u32[]{:S(2)}) async-start(bf16[128,4,128]{2,0,1:T(8,128)(2,1)} %broadcast_in_dim.20), calls=%async_computation.8 | async-start | bytes 262144 | tf_op jit(solution)/shard_map/all_to_all | solution.py:113
  509.0 12.3 %all-to-all-start.8 = ((bf16[128,4,128]{0,2,1:T(8,128)(2,1)}), bf16[128,4,128]{0,2,1:T(8,128)(2,1)S(1)}, u32[]{:S(2)}, u32[]{:S(2)}) async-start(bf16[128,4,128]{0,2,1:T(8,128)(2,1)} %broadcast_in_dim.22), calls=%async_computation.9 | async-start | bytes 262144 | tf_op jit(solution)/shard_map/all_to_all | solution.py:106
  521.3 25.4 %all-to-all-start.5 = ((bf16[128,4,1792]{0,2,1:T(8,128)(2,1)}), bf16[128,4,1792]{0,2,1:T(8,128)(2,1)}, u32[]{:S(2)}, u32[]{:S(2)}) async-start(bf16[128,4,1792]{0,2,1:T(8,128)(2,1)} %copy.46), calls=%async_computation.6 | async-start | bytes 3670016 | tf_op jit(solution)/shard_map/all_to_all | solution.py:92
  546.7 24.1 %all-to-all-start.9 = ((bf16[128,4,1792]{2,0,1:T(8,128)(2,1)}), bf16[128,4,1792]{2,0,1:T(8,128)(2,1)}, u32[]{:S(2)}, u32[]{:S(2)}) async-start(bf16[128,4,1792]{2,0,1:T(8,128)(2,1)} %fusion), calls=%async_computation.10 | async-start | bytes 3670016 | tf_op jit(solution)/shard_map/all_to_all | solution.py:99
  570.8 58.4 %all-to-all-start.3 = ((f32[32,4,896]{2,1,0:T(4,128)}), f32[32,4,896]{2,1,0:T(4,128)S(1)}, u32[]{:S(2)}, u32[]{:S(2)}) async-start(f32[32,4,896]{2,1,0:T(4,128)} %copy.43), calls=%async_computation.4 | async-start | bytes 917504 | tf_op jit(solution)/shard_map/all_to_all | solution.py:154
Sparse Core Ops, SparseCore 0:
  431.2 40.3 reduce-scatter.1
where the time goes:
time: 639 us; the launch traced here: 638 us
  waiting for transfers between devices  441 us (69%)
  starting transfers between devices  77.6 us (12%)
  local copies, waits for them, and re-layouts  47.5 us (7%)
  blocking collectives  30.1 us (5%)
  matrix products  20.7 us (3%)
  between operations  14.3 us (2%)
  other arithmetic  6.45 us (1%)
    all_to_all x1, waiting for transfers between devices, body(): lax.all_to_all(send_x.reshape(expert_count, capacity, width), 'dp', split...  163 us
    all_to_all x1, waiting for transfers between devices, body(): lax.all_to_all(send_dy.reshape(expert_count, capacity, width), 'dp', spli...  162 us
    all_to_all x1, waiting for transfers between devices, body(): lax.all_to_all(summed_grad.reshape(expert_count, capacity, share), 'dp',...  43.1 us
    all_to_all x1, starting transfers between devices, body(): lax.all_to_all(send_gate.reshape(expert_count, capacity), 'dp', split_axi...  28.7 us
    all_to_all x1, waiting for transfers between devices, body(): lax.all_to_all(summed_gate.reshape(expert_count, capacity), 'dp', split_a...  22.5 us
    unnamed x1, blocking collectives  21.7 us
    all_to_all x1, waiting for transfers between devices, body(): lax.all_to_all(scaled.reshape(slot_rows, local_count, column_width), 'loc...  17.5 us
    all_to_all x1, waiting for transfers between devices, body(): lax.all_to_all(send_gate.reshape(expert_count, capacity), 'dp', split_axi...  14.5 us
  transfers between devices with their start and end apart: 10, of which 8 were waited for; matrix products, arithmetic and copies ran while one was open for 9% of the time, Pallas kernels for 0%

commit v1 on v0

v1 whole, which is shorter than its diff:
```python
import functools

import jax
import jax.numpy as jnp
from jax import lax
from jax.experimental import pallas as pl
from jax.experimental.pallas import tpu as pltpu
from jax.sharding import PartitionSpec as P

F32 = jnp.float32
BF16 = jnp.bfloat16
MESH = pl.DeviceIdType.MESH
SLOTS = 128
RING = 4
LANES = 128


def dot(left, right, contract=(1, 0)):
    dims = (((contract[0],), (contract[1],)), ((), ()))
    return lax.dot_general(left, right, dims, preferred_element_type=F32)


def kernel(
    sizes,
    tok_ref,
    dy_ref,
    picks_ref,
    gates_ref,
    wg_hbm,
    wu_hbm,
    wd_hbm,
    in_grad_ref,
    gate_grad_ref,
    gg_hbm,
    gu_hbm,
    gd_hbm,
    own_chunk,
    got_chunk,
    own_meta,
    got_meta,
    ring,
    meta_tok,
    sel_tok,
    gate_slot,
    xd,
    wgu,
    wdn,
    part,
    part_in,
    hid,
    half_out,
    half_in,
    acc,
    acc_out,
    acc_in,
    gate_rows,
    dense,
    from_right,
    from_left,
    last_out,
    last_in,
    gg_buf,
    gu_buf,
    gd_buf,
    send_sem,
    recv_sem,
    zsend_sem,
    zrecv_sem,
    rsend_sem,
    rrecv_sem,
    local_sem,
):
    zs, top = sizes
    toks = 8 * zs
    half = own_chunk.shape[1]
    colw = 2 * half
    z = lax.axis_index("dp")
    n = lax.axis_index("node")
    x = lax.axis_index("local")
    y = n // 2
    c = n % 2
    zr, zl = (z + 1) % zs, (z + zs - 1) % zs
    xr, xl, xo = (x + 1) % RING, (x + 3) % RING, (x + 2) % RING
    yr, yl, yo = (y + 1) % RING, (y + 3) % RING, (y + 2) % RING
    nodes = 2 * RING
    sibling = (z, 2 * y + 1 - c, x)
    y_right, y_left = (z, 2 * yr + c, x), (z, 2 * yl + c, x)
    x_right, x_left = (z, n, xr), (z, n, xl)
    z_right, z_left = (zr, n, x), (zl, n, x)
    across = (z, 2 * x + c, y)
    moved = x != y

    count = [0]
    sends = []

    def remote(src, dst, device, keep=True):
        i = count[0]
        count[0] += 1
        copy = pltpu.make_async_remote_copy(
            src_ref=src,
            dst_ref=dst,
            send_sem=send_sem.at[i],
            recv_sem=recv_sem.at[i],
            device_id=device,
            device_id_type=MESH,
        )
        if keep:
            sends.append(copy)
        return copy

    row0 = pl.multiple_of(x * colw, LANES)
    loads = [
        pltpu.make_async_copy(
            wg_hbm.at[0, pl.ds(row0, colw), :], wgu.at[:, 0:LANES], local_sem.at[0]
        ),
        pltpu.make_async_copy(
            wu_hbm.at[0, pl.ds(row0, colw), :], wgu.at[:, LANES : 2 * LANES], local_sem.at[1]
        ),
        pltpu.make_async_copy(wd_hbm.at[0, :, pl.ds(row0, colw)], wdn, local_sem.at[2]),
    ]
    for load in loads:
        load.start()

    barrier = pltpu.get_barrier_semaphore()
    peers = [z_right, z_left]
    peers += [(z, n, (x + i) % RING) for i in range(1, RING)]
    peers += [(z, (n + i) % nodes, x) for i in range(1, nodes)]
    for peer in peers:
        pl.semaphore_signal(barrier, inc=1, device_id=peer, device_id_type=MESH)

    @pl.when(moved)
    def _():
        pl.semaphore_signal(barrier, inc=1, device_id=across, device_id_type=MESH)

    col0 = pl.multiple_of(y * colw + c * half, LANES)
    own_chunk[...] = jnp.concatenate(
        [tok_ref[:, pl.ds(col0, half)].astype(F32), dy_ref[:, pl.ds(col0, half)].astype(F32)],
        axis=0,
    ).astype(BF16)
    place = lax.broadcasted_iota(jnp.int32, (top, LANES), 0)
    lane_k = lax.broadcasted_iota(jnp.int32, (top, LANES), 1)
    put_picks = (lane_k == 32 * x + place).astype(F32).astype(BF16)
    put_gates = (lane_k == 32 * x + 8 + place).astype(F32).astype(BF16)
    meta = dot(picks_ref[...].astype(F32).astype(BF16), put_picks) + dot(gates_ref[...], put_gates)
    own_meta[...] = jnp.concatenate([meta, meta], axis=0).astype(BF16)
    got_meta[x] = own_meta[...]

    pl.semaphore_wait(barrier, len(peers) + jnp.where(moved, 1, 0))

    cross = remote(own_chunk, got_chunk, across, keep=False)

    @pl.when(moved)
    def _():
        cross.start()

    @pl.when(jnp.logical_not(moved))
    def _():
        got_chunk[...] = own_chunk[...]

    metas = [
        remote(own_meta, got_meta.at[x], (z, n, (x + i) % RING)) for i in range(1, RING)
    ]
    for copy in metas:
        copy.start()
    for copy in metas:
        copy.wait_recv()
    ring[0, :, half:] = (
        (got_meta[0].astype(F32) + got_meta[1].astype(F32))
        + (got_meta[2].astype(F32) + got_meta[3].astype(F32))
    ).astype(BF16)

    @pl.when(moved)
    def _():
        cross.wait_recv()

    ring[0, :, 0:half] = got_chunk[...]

    n_right = zs // 2
    n_left = zs - 1 - n_right

    def go_right(s):
        return pltpu.make_async_remote_copy(
            src_ref=ring.at[s],
            dst_ref=ring.at[s + 1],
            send_sem=zsend_sem.at[0, s],
            recv_sem=zrecv_sem.at[s + 1],
            device_id=z_right,
            device_id_type=MESH,
        )

    def go_left(s):
        return pltpu.make_async_remote_copy(
            src_ref=ring.at[(zs - s) % zs],
            dst_ref=ring.at[zs - 1 - s],
            send_sem=zsend_sem.at[1, s],
            recv_sem=zrecv_sem.at[zs - 1 - s],
            device_id=z_left,
            device_id_type=MESH,
        )

    go_right(0).start()
    if n_left > 0:
        go_left(0).start()

        def gather_step(s, carry):
            go_right(s - 1).wait_recv()
            go_right(s).start()
            go_left(s - 1).wait_recv()
            go_left(s).start()
            return carry

        lax.fori_loop(1, n_left, gather_step, 0)
        go_right(n_left - 1).wait_recv()
        go_right(n_left).start()
        go_left(n_left - 1).wait_recv()
    go_right(n_right - 1).wait_recv()

    meta_all = ring[:, :, half:].astype(F32)[:, 0:8, :].reshape(toks, LANES)
    meta_tok[...] = meta_all
    expert = z.astype(F32)
    t_row = lax.broadcasted_iota(jnp.int32, (toks, toks), 0)
    t_col = lax.broadcasted_iota(jnp.int32, (toks, toks), 1)
    before = jnp.logical_and(t_row // 8 == t_col // 8, t_col < t_row).astype(F32).astype(BF16)
    lane = lax.broadcasted_iota(jnp.int32, (toks, LANES), 1)
    t_of = lax.broadcasted_iota(jnp.int32, (toks, LANES), 0)

    def named(group):
        near = jnp.logical_and(lane >= 32 * group, lane < 32 * group + top)
        return jnp.logical_and(meta_all == expert, near)

    def select(group):
        chosen = jnp.sum(named(group).astype(F32), axis=1, keepdims=True)
        chosen = jnp.broadcast_to(chosen, (toks, LANES))
        rank = dot(before, chosen.astype(BF16))
        ok = jnp.logical_and(chosen > 0.5, rank == (lane % 4).astype(F32))
        return jnp.logical_and(ok, t_of // 8 == lane // 4).astype(F32)

    mine = select(y)
    cube = mine.reshape(zs, 8, SLOTS)
    blank = jnp.zeros_like(cube)
    pick_rows = jnp.concatenate(
        [jnp.concatenate([cube, blank], axis=2), jnp.concatenate([blank, cube], axis=2)], axis=1
    ).reshape(16 * zs, 2 * SLOTS)
    rows = ring[:, :, 0:half].reshape(16 * zs, half)
    picked = dot(pick_rows.astype(BF16), rows, (0, 0)).astype(BF16)
    xd[c, 0, y] = picked[0:SLOTS]
    xd[c, 1, y] = picked[SLOTS:]

    to_right = [remote(xd.at[c, p, y], xd.at[c, p, y], y_right) for p in range(2)]
    to_left = [remote(xd.at[c, p, y], xd.at[c, p, y], y_left) for p in range(2)]
    to_core = [remote(xd.at[c, p, y], xd.at[c, p, y], sibling) for p in range(2)]
    on_right = remote(xd.at[c, 0, yl], xd.at[c, 0, yl], y_right)
    on_left = remote(xd.at[c, 1, yr], xd.at[c, 1, yr], y_left)
    core_l = [remote(xd.at[c, p, yl], xd.at[c, p, yl], sibling) for p in range(2)]
    core_r = [remote(xd.at[c, p, yr], xd.at[c, p, yr], sibling) for p in range(2)]
    core_o = [remote(xd.at[c, p, yo], xd.at[c, p, yo], sibling) for p in range(2)]
    to_right[0].start()
    to_left[1].start()
    to_right[1].start()
    to_left[0].start()
    to_core[0].start()
    to_core[1].start()

    rolled = pltpu.roll(meta_all, LANES - 8, 1)
    for group in range(RING):
        chosen = select(group).astype(BF16)
        sel_tok[group] = chosen
        gate_of = jnp.sum(jnp.where(named(group), rolled, 0.0), axis=1, keepdims=True)
        gate_of = jnp.broadcast_to(gate_of, (toks, LANES)).astype(BF16)
        gate_slot[group] = dot(chosen, gate_of, (0, 0))

    to_right[0].wait_recv()
    on_right.start()
    core_l[0].start()
    to_left[1].wait_recv()
    on_left.start()
    core_r[1].start()
    to_right[1].wait_recv()
    core_l[1].start()
    to_left[0].wait_recv()
    core_r[0].start()
    on_right.wait_recv()
    core_o[0].start()
    on_left.wait_recv()
    core_o[1].start()
    for copy in to_core + core_l + core_r + core_o:
        copy.wait_recv()
    for load in loads:
        load.wait()

    n_slots = RING * SLOTS
    gate_up = dot(xd[0, 0].reshape(n_slots, half), wgu[0:half]) + dot(
        xd[1, 0].reshape(n_slots, half), wgu[half:]
    )
    back_part = dot(xd[0, 1].reshape(n_slots, half), wdn[:, 0:half], (1, 1)) + dot(
        xd[1, 1].reshape(n_slots, half), wdn[:, half:], (1, 1)
    )
    part[:, :, 0:256] = gate_up.reshape(RING, SLOTS, 256)
    part[:, :, 256:] = back_part.reshape(RING, SLOTS, LANES)

    lo, hi = slice(0, SLOTS // 2), slice(SLOTS // 2, SLOTS)

    def scatter_copies(src, into, r, l, o, right, left):
        return dict(
            a1=remote(src.at[o, lo], into.at[0, lo], right),
            b1=remote(src.at[o, hi], into.at[0, hi], left),
            a2=remote(src.at[r, hi], into.at[1, hi], right),
            b2=remote(src.at[l, lo], into.at[2, lo], left),
            a3=remote(src.at[r, lo], into.at[1, lo], right),
            b3=remote(src.at[l, hi], into.at[2, hi], left),
        )

    px = scatter_copies(part, part_in, xr, xl, xo, x_right, x_left)
    px["a1"].start()
    px["b1"].start()
    px["a2"].start()
    px["b2"].start()
    px["a1"].wait_recv()
    part[xr, lo] = part[xr, lo] + part_in[0, lo]
    px["a3"].start()
    px["b1"].wait_recv()
    part[xl, hi] = part[xl, hi] + part_in[0, hi]
    px["b3"].start()
    for name in ("a2", "b2", "a3", "b3"):
        px[name].wait_recv()
    summed = part[x] + part_in[1] + part_in[2]

    gate_pre = summed[:, 0:128]
    up_pre = summed[:, 128:256]
    back = summed[:, 256:384]
    gate_col = gate_slot[x]
    sig = jax.nn.sigmoid(gate_pre)
    act = gate_pre * sig * up_pre
    d_act = gate_col * back
    d_up = d_act * gate_pre * sig
    d_pre = d_act * up_pre * sig * (1.0 + gate_pre * (1.0 - sig))
    hid[x, :, 0:128] = d_pre.astype(BF16)
    hid[x, :, 128:256] = d_up.astype(BF16)
    hid[x, :, 256:384] = act.astype(BF16)

    h_right = remote(hid.at[x], hid.at[x], x_right)
    h_left = remote(hid.at[x], hid.at[x], x_left)
    h_on_right = remote(hid.at[xl, lo], hid.at[xl, lo], x_right)
    h_on_left = remote(hid.at[xr, hi], hid.at[xr, hi], x_left)
    h_right.start()
    h_left.start()

    gate_row = jnp.sum(jnp.transpose(back * act), axis=0, keepdims=True)
    gate_rows[n] = jnp.broadcast_to(gate_row, (8, SLOTS))
    rows_out = [
        remote(gate_rows.at[n], gate_rows.at[n], (z, (n + i) % nodes, x)) for i in range(1, nodes)
    ]
    for copy in rows_out:
        copy.start()

    h_right.wait_recv()
    h_on_right.start()
    h_left.wait_recv()
    h_on_left.start()
    h_on_right.wait_recv()
    h_on_left.wait_recv()

    grads = hid[:, :, 0:256].reshape(n_slots, 256)
    other = pl.multiple_of((1 - c) * half, LANES)
    ours = pl.multiple_of(c * half, LANES)
    half_out[...] = dot(grads, wgu[pl.ds(other, half), :], (1, 1)).astype(BF16)
    core_half = remote(half_out, half_in, sibling)
    core_half.start()
    acc[...] = dot(grads, wgu[pl.ds(ours, half), :], (1, 1)).reshape(RING, SLOTS, half)
    core_half.wait_recv()
    arrived = half_in[...].astype(F32).reshape(RING, SLOTS, half)
    acc[...] = acc[...] + arrived

    py = scatter_copies(acc_out, acc_in, yr, yl, yo, y_right, y_left)
    acc_out[yo] = acc[yo].astype(BF16)
    py["a1"].start()
    py["b1"].start()
    acc_out[yr, hi] = acc[yr, hi].astype(BF16)
    py["a2"].start()
    acc_out[yl, lo] = acc[yl, lo].astype(BF16)
    py["b2"].start()

    for copy in rows_out:
        copy.wait_recv()
    gate_sum = gate_rows[0]
    for i in range(1, nodes):
        gate_sum = gate_sum + gate_rows[i]
    gate_tok = jnp.sum(sel_tok[x].astype(F32) * gate_sum[0:1], axis=1, keepdims=True)
    meta_x = jnp.zeros((toks, LANES), F32)
    for i in range(RING):
        turned = meta_tok[...] if i == 0 else pltpu.roll(meta_tok[...], LANES - 32 * i, 1)
        meta_x = jnp.where(x == i, turned, meta_x)
    hit = jnp.logical_and(meta_x == expert, lane < top)
    dense[:, :, half:] = jnp.where(hit, gate_tok, 0.0).reshape(zs, 8, LANES)

    py["a1"].wait_recv()
    acc_out[yr, lo] = (acc[yr, lo] + acc_in[0, lo].astype(F32)).astype(BF16)
    py["a3"].start()
    py["b1"].wait_recv()
    acc_out[yl, hi] = (acc[yl, hi] + acc_in[0, hi].astype(F32)).astype(BF16)
    py["b3"].start()
    for name in ("a2", "b2", "a3", "b3"):
        py[name].wait_recv()
    total = acc[y] + acc_in[1].astype(F32) + acc_in[2].astype(F32)

    sel = sel_tok[y]
    first = total.astype(BF16)
    rest = total - first.astype(F32)
    second = rest.astype(BF16)
    third = (rest - second.astype(F32)).astype(BF16)
    spread = dot(sel, first) + (dot(sel, second) + dot(sel, third))
    dense[:, :, 0:half] = spread.reshape(zs, 8, half)

    def sum_left(s):
        return pltpu.make_async_remote_copy(
            src_ref=dense.at[n_right - s],
            dst_ref=from_right.at[n_right - 1 - s],
            send_sem=rsend_sem.at[0, s],
            recv_sem=rrecv_sem.at[0, s],
            device_id=z_left,
            device_id_type=MESH,
        )

    def sum_right(s):
        return pltpu.make_async_remote_copy(
            src_ref=dense.at[zs - n_left + s],
            dst_ref=from_left.at[s],
            send_sem=rsend_sem.at[1, s],
            recv_sem=rrecv_sem.at[1, s],
            device_id=z_right,
            device_id_type=MESH,
        )

    tiles = colw // LANES
    per = -(-tiles // max(1, n_right - 1))

    def weight_tile(t):
        side = t // (half // LANES)
        at = pl.multiple_of((t % (half // LANES)) * LANES, LANES)
        down = pl.multiple_of(t * LANES, LANES)
        xs = xd[side, 0, :, :, pl.ds(at, LANES)].reshape(n_slots, LANES)
        ds = xd[side, 1, :, :, pl.ds(at, LANES)].astype(F32)
        scaled = (gate_slot[...] * ds).astype(BF16).reshape(n_slots, LANES)
        both = dot(xs, hid[:, :, 0:256].reshape(n_slots, 256), (0, 0)).astype(BF16)
        gg_buf[pl.ds(down, LANES), :] = both[:, 0:128]
        gu_buf[pl.ds(down, LANES), :] = both[:, 128:256]
        gd_buf[:, pl.ds(down, LANES)] = dot(
            hid[:, :, 256:384].reshape(n_slots, LANES), scaled, (0, 0)
        ).astype(BF16)

    sum_left(0).start()
    if n_left > 0:
        sum_right(0).start()

    def sum_step(s, carry):
        sum_left(s - 1).wait_recv()
        dense[n_right - s] = dense[n_right - s] + from_right[n_right - s]
        sum_left(s).start()

        @pl.when(s < n_left)
        def _():
            sum_right(s - 1).wait_recv()
            dense[zs - n_left + s] = dense[zs - n_left + s] + from_left[s - 1]
            sum_right(s).start()

        for q in range(per):
            t = (s - 1) * per + q

            @pl.when(t < tiles)
            def _():
                weight_tile(t)

        return carry

    if n_right > 1:
        lax.fori_loop(1, n_right, sum_step, 0)
    else:
        lax.fori_loop(0, tiles, lambda t, carry: (weight_tile(t), carry)[1], 0)
    stores = [
        pltpu.make_async_copy(gg_buf, gg_hbm.at[0], local_sem.at[0]),
        pltpu.make_async_copy(gu_buf, gu_hbm.at[0], local_sem.at[1]),
        pltpu.make_async_copy(gd_buf, gd_hbm.at[0], local_sem.at[2]),
    ]
    for store in stores:
        store.start()
    sum_left(n_right - 1).wait_recv()
    final = dense[0] + from_right[0]
    if n_left > 0:
        sum_right(n_left - 1).wait_recv()
        final = final + from_left[n_left - 1]
    gate_grad_ref[...] = final[:, half:]
    last_out[...] = final[:, 0:half]
    end = remote(last_out, last_in, across, keep=False)

    @pl.when(moved)
    def _():
        end.start()
        end.wait_recv()

    @pl.when(jnp.logical_not(moved))
    def _():
        last_in[...] = last_out[...]

    in_grad_ref[...] = last_in[...].astype(BF16)

    @pl.when(moved)
    def _():
        cross.wait_send()
        end.wait_send()

    for copy in sends:
        copy.wait_send()

    def drain_right(s, carry):
        go_right(s).wait_send()
        sum_left(s).wait_send()
        return carry

    def drain_left(s, carry):
        go_left(s).wait_send()
        sum_right(s).wait_send()
        return carry

    lax.fori_loop(0, n_right, drain_right, 0)
    if n_left > 0:
        lax.fori_loop(0, n_left, drain_left, 0)
    for store in stores:
        store.wait()


def body(tokens, out_grad, picks, gates, w_gate, w_up, w_down):
    zs = lax.axis_size("dp")
    width = tokens.shape[1]
    top = picks.shape[1]
    half = width // (2 * RING)
    colw = 2 * half
    toks = 8 * zs
    n_right = zs // 2
    any_spec = pl.BlockSpec(memory_space=pl.ANY)
    vmem_spec = pl.BlockSpec(memory_space=pltpu.VMEM)
    in_grad, gate_grad, gg, gu, gd = pl.pallas_call(
        functools.partial(kernel, (zs, top)),
        out_shape=(
            jax.ShapeDtypeStruct((8, half), BF16),
            jax.ShapeDtypeStruct((8, LANES), F32),
            jax.ShapeDtypeStruct((1, colw, LANES), BF16),
            jax.ShapeDtypeStruct((1, colw, LANES), BF16),
            jax.ShapeDtypeStruct((1, LANES, colw), BF16),
        ),
        in_specs=[vmem_spec] * 4 + [any_spec] * 3,
        out_specs=(vmem_spec, vmem_spec, any_spec, any_spec, any_spec),
        scratch_shapes=[
            pltpu.VMEM((16, half), BF16),
            pltpu.VMEM((16, half), BF16),
            pltpu.VMEM((16, LANES), BF16),
            pltpu.VMEM((RING, 16, LANES), BF16),
            pltpu.VMEM((zs, 16, half + LANES), BF16),
            pltpu.VMEM((toks, LANES), F32),
            pltpu.VMEM((RING, toks, SLOTS), BF16),
            pltpu.VMEM((RING, SLOTS, LANES), F32),
            pltpu.VMEM((2, 2, RING, SLOTS, half), BF16),
            pltpu.VMEM((colw, 2 * LANES), BF16),
            pltpu.VMEM((LANES, colw), BF16),
            pltpu.VMEM((RING, SLOTS, 3 * LANES), F32),
            pltpu.VMEM((3, SLOTS, 3 * LANES), F32),
            pltpu.VMEM((RING, SLOTS, 3 * LANES), BF16),
            pltpu.VMEM((RING * SLOTS, half), BF16),
            pltpu.VMEM((RING * SLOTS, half), BF16),
            pltpu.VMEM((RING, SLOTS, half), F32),
            pltpu.VMEM((RING, SLOTS, half), BF16),
            pltpu.VMEM((3, SLOTS, half), BF16),
            pltpu.VMEM((2 * RING, 8, SLOTS), F32),
            pltpu.VMEM((zs, 8, half + LANES), F32),
            pltpu.VMEM((n_right, 8, half + LANES), F32),
            pltpu.VMEM((n_right, 8, half + LANES), F32),
            pltpu.VMEM((8, half), F32),
            pltpu.VMEM((8, half), F32),
            pltpu.VMEM((colw, LANES), BF16),
            pltpu.VMEM((colw, LANES), BF16),
            pltpu.VMEM((LANES, colw), BF16),
            pltpu.SemaphoreType.DMA((48,)),
            pltpu.SemaphoreType.DMA((48,)),
            pltpu.SemaphoreType.DMA((2, n_right)),
            pltpu.SemaphoreType.DMA((zs,)),
            pltpu.SemaphoreType.DMA((2, n_right)),
            pltpu.SemaphoreType.DMA((2, n_right)),
            pltpu.SemaphoreType.DMA((3,)),
        ],
        compiler_params=pltpu.CompilerParams(
            collective_id=0, has_side_effects=True, vmem_limit_bytes=48 * 1024 * 1024
        ),
    )(tokens, out_grad, picks, gates, w_gate, w_up, w_down)
    return in_grad, gate_grad[:, 0:top], gg, gu, gd


def solution(mesh):
    placed = (
        P(("dp", "local"), None),
        P(("dp", "local"), None),
        P(("dp", "local"), None),
        P(("dp", "local"), None),
        P("dp", None, "node"),
        P("dp", None, "node"),
        P("dp", "node", None),
    )
    return jax.shard_map(
        body,
        mesh=mesh,
        in_specs=placed,
        out_specs=(
            P(("dp", "local"), "node"),
            P(("dp", "local"), None),
            P("dp", "local", "node"),
            P("dp", "local", "node"),
            P("dp", "node", "local"),
        ),
        check_vma=False,
    )
```

time: 639 us -> 185 us (0.29)
  waiting for transfers between devices: 441 us -> 0 us
  Pallas kernels: 0 us -> 174 us
  starting transfers between devices: 77.6 us -> 0 us
  local copies, waits for them, and re-layouts: 47.5 us -> 9.65 us
  blocking collectives: 30.1 us -> 0 us
  matrix products: 20.7 us -> 0 us
  between operations: 14.3 us -> 0.66 us
  other arithmetic: 6.45 us -> 0 us
    all_to_all x9 -> x0, waiting for transfers between devices: 441 us -> none  [the longest x1 163 us: body(): lax.all_to_all(send_x.reshape(expert_count, capacity, width), 'dp', split...]
    pallas_call x0 -> x1, Pallas kernels: none -> 174 us  [body(): pl.pallas_call(functools.partial(kernel, (zs, top)), out_shape=(jax.Shape...]
    all_to_all x9 -> x0, starting transfers between devices: 77.6 us -> none  [the longest x1 28.7 us: body(): lax.all_to_all(send_gate.reshape(expert_count, capacity), 'dp', split_axi...]
    reshape x11 -> x0, local copies, waits for them, and re-layouts: 24.7 us -> none  [the longest x1 4.1 us: body(): send_x.reshape(expert_count, capacity, width)]
    unnamed x1 -> x0, blocking collectives: 21.7 us -> none
    dot_general x11 -> x0, matrix products: 20.7 us -> none  [the longest x3 8.5 us: contract_first(): lax.dot_general(left, right, (((0,), (0,)), ((), ())), preferred_element_...]
    another operation x2 -> x0, local copies, waits for them, and re-layouts: 8.99 us -> none  [body(): arrived_x.reshape(slot_rows, local_count, column_width)]
    all_to_all x1 -> x0, blocking collectives: 8.36 us -> none  [body(): lax.all_to_all(jnp.broadcast_to(d_pre[:, None, :], spread), 'local', spli...]
  transfers between devices with their start and end apart: 10 -> 0, of which waited for: 8 -> 0; matrix products, arithmetic and copies ran while one was open for 9% -> 0% of each run, Pallas kernels for 0% -> 0%
where the time goes in v1:
time: 185 us; the launch traced here: 184 us
  Pallas kernels  174 us (94%)
  local copies, waits for them, and re-layouts  9.65 us (5%)
    pallas_call x1, Pallas kernels, body(): pl.pallas_call(functools.partial(kernel, (zs, top)), out_shape=(jax.Shape...  174 us
    unnamed x17, local copies, waits for them, and re-layouts  9.65 us

profile of v1, /device:TPU:24, one launch (start us, length us, event | category | flops | bytes accessed | tf_op | source)
XLA Modules:
  0.0 184.1 jit_solution(17724802270142045862)
XLA Ops:
  0.6 0.0 copy-start
  0.6 1.5 copy-done
  2.1 0.0 copy-start.1
  2.1 1.5 copy-done.1
  3.6 0.0 copy-start.2
  3.6 0.9 copy-done.2
  4.5 0.0 copy-start.3
  4.5 0.9 copy-done.3
  5.4 0.0 copy-start.4
  5.4 0.7 copy-done.4
  6.1 0.0 copy-start.5
  6.1 0.7 copy-done.5
  6.8 173.8 %shard_map.110 = (bf16[8,896]{1,0:T(8,128)(2,1)S(1)}, f32[8,128]{1,0:T(8,128)S(1)}, bf16[1,1792,128]{2,1,0:T(8,128)(2,1)S(1)}, bf16[1,1792,128]{2,1,0:T(8,128)(2,1)S(1)}, bf16[1,128,1792]{2,1,0:T(8,128)(2,1)S(1)}) custom-call(bf16[8,7168]{1,0:T(8,128)(2,1)S(1)} %copy-done.2, bf16[8,7168]{1,0:T(8,128)(2,1)S(1)} %copy-done.3, s32[8,8]{1,0:T(8,128)S(1)} %copy-done.4, ...), custom_call_target="tpu_custom_call" | custom-call | tf_op jit(solution)/shard_map/pallas_call | solution.py:541
  180.6 0.6 copy.17
  181.2 0.6 copy.18
  181.8 0.8 copy.19
  182.5 0.8 copy.20
  183.3 0.8 copy.21
Async XLA Ops:
  0.6 1.5 copy-start
  2.1 1.5 copy-start.1
  3.6 0.9 copy-start.2
  4.5 0.9 copy-start.3
  5.4 0.7 copy-start.4
  6.1 0.7 copy-start.5

commit v2 on v1

--- a/solution.py
+++ b/solution.py
@@ -13,6 +13,28 @@
 SLOTS = 128
 RING = 4
 LANES = 128
+
+
+HOP = 5
+
+
+def plan(zs):
+    far, near = zs // 2, -(zs - 1 - zs // 2)
+    stops = [0]
+    for j in range(1, far // HOP + 1):
+        stops += [d for d in (HOP * j, -HOP * j) if near <= d <= far]
+    seen = set(stops)
+    serves = {}
+    for stop in stops:
+        serves[stop] = []
+        for step in range(1, HOP // 2 + 1):
+            for off in (step, -step):
+                d = stop + off
+                if near <= d <= far and d not in seen:
+                    seen.add(d)
+                    serves[stop].append(off)
+    assert len(seen) == zs
+    return stops, serves
 
 
 def dot(left, right, contract=(1, 0)):
@@ -31,9 +53,9 @@
     wd_hbm,
     in_grad_ref,
     gate_grad_ref,
-    gg_hbm,
-    gu_hbm,
-    gd_hbm,
+    gg_ref,
+    gu_ref,
+    gd_ref,
     own_chunk,
     got_chunk,
     own_meta,
@@ -55,19 +77,13 @@
     acc_in,
     gate_rows,
     dense,
-    from_right,
-    from_left,
+    dense_out,
+    near_in,
+    far_in,
     last_out,
     last_in,
-    gg_buf,
-    gu_buf,
-    gd_buf,
     send_sem,
     recv_sem,
-    zsend_sem,
-    zrecv_sem,
-    rsend_sem,
-    rrecv_sem,
     local_sem,
 ):
     zs, top = sizes
@@ -79,14 +95,14 @@
     x = lax.axis_index("local")
     y = n // 2
     c = n % 2
-    zr, zl = (z + 1) % zs, (z + zs - 1) % zs
+    stops, serves = plan(zs)
+    offsets = sorted({off for stop in stops for off in serves[stop]} | {HOP, -HOP})
     xr, xl, xo = (x + 1) % RING, (x + 3) % RING, (x + 2) % RING
     yr, yl, yo = (y + 1) % RING, (y + 3) % RING, (y + 2) % RING
     nodes = 2 * RING
     sibling = (z, 2 * y + 1 - c, x)
     y_right, y_left = (z, 2 * yr + c, x), (z, 2 * yl + c, x)
     x_right, x_left = (z, n, xr), (z, n, xl)
-    z_right, z_left = (zr, n, x), (zl, n, x)
     across = (z, 2 * x + c, y)
     moved = x != y
 
@@ -122,7 +138,7 @@
         load.start()
 
     barrier = pltpu.get_barrier_semaphore()
-    peers = [z_right, z_left]
+    peers = [((z + off + zs) % zs, n, x) for off in offsets]
     peers += [(z, n, (x + i) % RING) for i in range(1, RING)]
     peers += [(z, (n + i) % nodes, x) for i in range(1, nodes)]
     for peer in peers:
@@ -175,45 +191,24 @@
 
     ring[0, :, 0:half] = got_chunk[...]
 
-    n_right = zs // 2
-    n_left = zs - 1 - n_right
-
-    def go_right(s):
-        return pltpu.make_async_remote_copy(
-            src_ref=ring.at[s],
-            dst_ref=ring.at[s + 1],
-            send_sem=zsend_sem.at[0, s],
-            recv_sem=zrecv_sem.at[s + 1],
-            device_id=z_right,
-            device_id_type=MESH,
-        )
-
-    def go_left(s):
-        return pltpu.make_async_remote_copy(
-            src_ref=ring.at[(zs - s) % zs],
-            dst_ref=ring.at[zs - 1 - s],
-            send_sem=zsend_sem.at[1, s],
-            recv_sem=zrecv_sem.at[zs - 1 - s],
-            device_id=z_left,
-            device_id_type=MESH,
-        )
-
-    go_right(0).start()
-    if n_left > 0:
-        go_left(0).start()
-
-        def gather_step(s, carry):
-            go_right(s - 1).wait_recv()
-            go_right(s).start()
-            go_left(s - 1).wait_recv()
-            go_left(s).start()
-            return carry
-
-        lax.fori_loop(1, n_left, gather_step, 0)
-        go_right(n_left - 1).wait_recv()
-        go_right(n_left).start()
-        go_left(n_left - 1).wait_recv()
-    go_right(n_right - 1).wait_recv()
+    coming = {}
+
+    def pass_on(d, off):
+        copy = remote(ring.at[d % zs], ring.at[(d + off) % zs], ((z + off + zs) % zs, n, x))
+        copy.start()
+        coming[d + off] = copy
+
+    for stop in stops:
+        if stop != 0:
+            coming[stop].wait_recv()
+        for step in (HOP, -HOP):
+            if stop * step >= 0 and stop + step in stops:
+                pass_on(stop, step)
+        for off in serves[stop]:
+            pass_on(stop, off)
+    for d in coming:
+        if d not in stops:
+            coming[d].wait_recv()
 
     meta_all = ring[:, :, half:].astype(F32)[:, 0:8, :].reshape(toks, LANES)
     meta_tok[...] = meta_all
@@ -391,7 +386,10 @@
         turned = meta_tok[...] if i == 0 else pltpu.roll(meta_tok[...], LANES - 32 * i, 1)
         meta_x = jnp.where(x == i, turned, meta_x)
     hit = jnp.logical_and(meta_x == expert, lane < top)
-    dense[:, :, half:] = jnp.where(hit, gate_tok, 0.0).reshape(zs, 8, LANES)
+    gate_hi = gate_tok.astype(BF16).astype(F32)
+    gate_tile = jnp.where(hit, gate_hi, 0.0) + pltpu.roll(
+        jnp.where(hit, gate_tok - gate_hi, 0.0), LANES // 2, 1
+    )
 
     py["a1"].wait_recv()
     acc_out[yr, lo] = (acc[yr, lo] + acc_in[0, lo].astype(F32)).astype(BF16)
@@ -409,31 +407,24 @@
     second = rest.astype(BF16)
     third = (rest - second.astype(F32)).astype(BF16)
     spread = dot(sel, first) + (dot(sel, second) + dot(sel, third))
-    dense[:, :, 0:half] = spread.reshape(zs, 8, half)
-
-    def sum_left(s):
-        return pltpu.make_async_remote_copy(
-            src_ref=dense.at[n_right - s],
-            dst_ref=from_right.at[n_right - 1 - s],
-            send_sem=rsend_sem.at[0, s],
-            recv_sem=rrecv_sem.at[0, s],
-            device_id=z_left,
-            device_id_type=MESH,
-        )
-
-    def sum_right(s):
-        return pltpu.make_async_remote_copy(
-            src_ref=dense.at[zs - n_left + s],
-            dst_ref=from_left.at[s],
-            send_sem=rsend_sem.at[1, s],
-            recv_sem=rrecv_sem.at[1, s],
-            device_id=z_right,
-            device_id_type=MESH,
-        )
+    full = jnp.concatenate([spread, gate_tile], axis=1)
+    wide = (half + LANES) // 2
+    dense[:, 0:8, :] = full[:, 0:wide].reshape(zs, 8, wide)
+    dense[:, 8:16, :] = full[:, wide:].reshape(zs, 8, wide)
+    dense_out[...] = dense[...].astype(BF16)
+
+    near = {}
+    for stop in reversed(stops):
+        for off in serves[stop]:
+            near[stop, off] = remote(
+                dense_out.at[(stop + off) % zs],
+                near_in.at[len(near)],
+                ((z - off + zs) % zs, n, x),
+            )
+            near[stop, off].start()
+    slot_of = {key: i for i, key in enumerate(near)}
 
     tiles = colw // LANES
-    per = -(-tiles // max(1, n_right - 1))
-
     def weight_tile(t):
         side = t // (half // LANES)
         at = pl.multiple_of((t % (half // LANES)) * LANES, LANES)
@@ -442,53 +433,49 @@
         ds = xd[side, 1, :, :, pl.ds(at, LANES)].astype(F32)
         scaled = (gate_slot[...] * ds).astype(BF16).reshape(n_slots, LANES)
         both = dot(xs, hid[:, :, 0:256].reshape(n_slots, 256), (0, 0)).astype(BF16)
-        gg_buf[pl.ds(down, LANES), :] = both[:, 0:128]
-        gu_buf[pl.ds(down, LANES), :] = both[:, 128:256]
-        gd_buf[:, pl.ds(down, LANES)] = dot(
+        gg_ref[0, pl.ds(down, LANES), :] = both[:, 0:128]
+        gu_ref[0, pl.ds(down, LANES), :] = both[:, 128:256]
+        gd_ref[0, :, pl.ds(down, LANES)] = dot(
             hid[:, :, 256:384].reshape(n_slots, LANES), scaled, (0, 0)
         ).astype(BF16)
 
-    sum_left(0).start()
-    if n_left > 0:
-        sum_right(0).start()
-
-    def sum_step(s, carry):
-        sum_left(s - 1).wait_recv()
-        dense[n_right - s] = dense[n_right - s] + from_right[n_right - s]
-        sum_left(s).start()
-
-        @pl.when(s < n_left)
-        def _():
-            sum_right(s - 1).wait_recv()
-            dense[zs - n_left + s] = dense[zs - n_left + s] + from_left[s - 1]
-            sum_right(s).start()
-
-        for q in range(per):
-            t = (s - 1) * per + q
-
-            @pl.when(t < tiles)
-            def _():
-                weight_tile(t)
-
-        return carry
-
-    if n_right > 1:
-        lax.fori_loop(1, n_right, sum_step, 0)
-    else:
-        lax.fori_loop(0, tiles, lambda t, carry: (weight_tile(t), carry)[1], 0)
-    stores = [
-        pltpu.make_async_copy(gg_buf, gg_hbm.at[0], local_sem.at[0]),
-        pltpu.make_async_copy(gu_buf, gu_hbm.at[0], local_sem.at[1]),
-        pltpu.make_async_copy(gd_buf, gd_hbm.at[0], local_sem.at[2]),
-    ]
-    for store in stores:
-        store.start()
-    sum_left(n_right - 1).wait_recv()
-    final = dense[0] + from_right[0]
-    if n_left > 0:
-        sum_right(n_left - 1).wait_recv()
-        final = final + from_left[n_left - 1]
-    gate_grad_ref[...] = final[:, half:]
+    def weight_tiles(first, last):
+        def one(t, carry):
+            weight_tile(t)
+            return carry
+
+        lax.fori_loop(first, last, one, 0)
+
+    levels = len(stops) // 2
+    share = -(-tiles // (levels + 1))
+    weight_tiles(0, min(share, tiles))
+    far = {}
+    for i, stop in enumerate(reversed(stops)):
+        value = dense[stop % zs]
+        for off in serves[stop]:
+            near[stop, off].wait_recv()
+            value = value + near_in[slot_of[stop, off]].astype(F32)
+        for step in (HOP, -HOP):
+            if stop * step >= 0 and stop + step in stops:
+                far[stop + step].wait_recv()
+                value = value + far_in[stops.index(stop + step) - 1].astype(F32)
+        if stop == 0:
+            final = value
+        else:
+            dense_out[stop % zs] = value.astype(BF16)
+            back_by = HOP if stop > 0 else -HOP
+            far[stop] = remote(
+                dense_out.at[stop % zs],
+                far_in.at[stops.index(stop) - 1],
+                ((z - back_by + zs) % zs, n, x),
+            )
+            far[stop].start()
+            if i % 2 == 1:
+                done = share * ((i + 1) // 2)
+                weight_tiles(min(done, tiles), min(done + share, tiles))
+    final = jnp.concatenate([final[0:8], final[8:16]], axis=1)
+    gate_both = final[:, half:]
+    gate_grad_ref[...] = gate_both + pltpu.roll(gate_both, LANES // 2, 1)
     last_out[...] = final[:, 0:half]
     end = remote(last_out, last_in, across, keep=False)
 
@@ -510,22 +497,6 @@
 
     for copy in sends:
         copy.wait_send()
-
-    def drain_right(s, carry):
-        go_right(s).wait_send()
-        sum_left(s).wait_send()
-        return carry
-
-    def drain_left(s, carry):
-        go_left(s).wait_send()
-        sum_right(s).wait_send()
-        return carry
-
-    lax.fori_loop(0, n_right, drain_right, 0)
-    if n_left > 0:
-        lax.fori_loop(0, n_left, drain_left, 0)
-    for store in stores:
-        store.wait()
 
 
 def body(tokens, out_grad, picks, gates, w_gate, w_up, w_down):
@@ -535,8 +506,9 @@
     half = width // (2 * RING)
     colw = 2 * half
     toks = 8 * zs
-    n_right = zs // 2
-    any_spec = pl.BlockSpec(memory_space=pl.ANY)
+    wide = (half + LANES) // 2
+    stops, _ = plan(zs)
+    hbm_spec = pl.BlockSpec(memory_space=pltpu.HBM)
     vmem_spec = pl.BlockSpec(memory_space=pltpu.VMEM)
     in_grad, gate_grad, gg, gu, gd = pl.pallas_call(
         functools.partial(kernel, (zs, top)),
@@ -547,8 +519,8 @@
             jax.ShapeDtypeStruct((1, colw, LANES), BF16),
             jax.ShapeDtypeStruct((1, LANES, colw), BF16),
         ),
-        in_specs=[vmem_spec] * 4 + [any_spec] * 3,
-        out_specs=(vmem_spec, vmem_spec, any_spec, any_spec, any_spec),
+        in_specs=[vmem_spec] * 4 + [hbm_spec] * 3,
+        out_specs=(vmem_spec,) * 5,
         scratch_shapes=[
             pltpu.VMEM((16, half), BF16),
             pltpu.VMEM((16, half), BF16),
@@ -570,24 +542,18 @@
             pltpu.VMEM((RING, SLOTS, half), BF16),
             pltpu.VMEM((3, SLOTS, half), BF16),
             pltpu.VMEM((2 * RING, 8, SLOTS), F32),
-            pltpu.VMEM((zs, 8, half + LANES), F32),
-            pltpu.VMEM((n_right, 8, half + LANES), F32),
-            pltpu.VMEM((n_right, 8, half + LANES), F32),
+            pltpu.VMEM((zs, 16, wide), F32),
+            pltpu.VMEM((zs, 16, wide), BF16),
+            pltpu.VMEM((zs - len(stops), 16, wide), BF16),
+            pltpu.VMEM((len(stops) - 1, 16, wide), BF16),
             pltpu.VMEM((8, half), F32),
             pltpu.VMEM((8, half), F32),
-            pltpu.VMEM((colw, LANES), BF16),
-            pltpu.VMEM((colw, LANES), BF16),
-            pltpu.VMEM((LANES, colw), BF16),
-            pltpu.SemaphoreType.DMA((48,)),
-            pltpu.SemaphoreType.DMA((48,)),
-            pltpu.SemaphoreType.DMA((2, n_right)),
-            pltpu.SemaphoreType.DMA((zs,)),
-            pltpu.SemaphoreType.DMA((2, n_right)),
-            pltpu.SemaphoreType.DMA((2, n_right)),
+            pltpu.SemaphoreType.DMA((48 + 2 * zs,)),
+            pltpu.SemaphoreType.DMA((48 + 2 * zs,)),
             pltpu.SemaphoreType.DMA((3,)),
         ],
         compiler_params=pltpu.CompilerParams(
-            collective_id=0, has_side_effects=True, vmem_limit_bytes=48 * 1024 * 1024
+            collective_id=0, has_side_effects=True, vmem_limit_bytes=60 * 1024 * 1024
         ),
     )(tokens, out_grad, picks, gates, w_gate, w_up, w_down)
     return in_grad, gate_grad[:, 0:top], gg, gu, gd

time: 185 us -> 140 us (0.76)
  Pallas kernels: 174 us -> 131 us
  local copies, waits for them, and re-layouts: 9.65 us -> 7.03 us
    pallas_call x1, Pallas kernels: 174 us -> 131 us  [body(): pl.pallas_call(functools.partial(kernel, (zs, top)), out_shape=(jax.Shape...]
    unnamed x17 -> x7, local copies, waits for them, and re-layouts: 9.65 us -> 7.03 us
where the time goes in v2:
time: 140 us; the launch traced here: 139 us
  Pallas kernels  131 us (94%)
  local copies, waits for them, and re-layouts  7.03 us (5%)
    pallas_call x1, Pallas kernels, body(): pl.pallas_call(functools.partial(kernel, (zs, top)), out_shape=(jax.Shape...  131 us
    unnamed x7, local copies, waits for them, and re-layouts  7.03 us

profile of v2, /device:TPU:24, one launch (start us, length us, event | category | flops | bytes accessed | tf_op | source)
XLA Modules:
  0.0 139.1 jit_solution(6042155297363216547)
XLA Ops:
  0.6 131.4 %shard_map.110 = (bf16[8,896]{1,0:T(8,128)(2,1)}, f32[8,128]{1,0:T(8,128)}, bf16[1,1792,128]{2,1,0:T(8,128)(2,1)}, bf16[1,1792,128]{2,1,0:T(8,128)(2,1)}, bf16[1,128,1792]{2,1,0:T(8,128)(2,1)}) custom-call(bf16[8,7168]{1,0:T(8,128)(2,1)} %tok_ref.1, bf16[8,7168]{1,0:T(8,128)(2,1)} %dy_ref.1, s32[8,8]{1,0:T(8,128)} %picks_ref.1, bf16[8,8]{1,0:T(8,128)(2,1)} %gates_ref.1, ...), custom_call_target="tpu_custom_call" | custom-call | tf_op jit(solution)/shard_map/pallas_call | solution.py:513
  132.0 0.0 copy-start
  132.0 1.4 copy.17
  133.4 1.3 copy.18
  134.7 1.8 %copy.19 = bf16[1,1792,128]{2,1,0:T(8,128)(2,1)} copy(bf16[1,1792,128]{2,1,0:T(8,128)(2,1)} %get-tuple-element.22) | data formatting | bytes 917504
  136.5 1.8 %copy.20 = bf16[1,1792,128]{2,1,0:T(8,128)(2,1)} copy(bf16[1,1792,128]{2,1,0:T(8,128)(2,1)} %get-tuple-element.23) | data formatting | bytes 917504
  138.3 0.0 copy-done
  138.3 0.8 copy.21
Async XLA Ops:
  132.0 6.3 %copy-start = (bf16[1,128,1792]{2,1,0:T(8,128)(2,1)S(1)}, bf16[1,128,1792]{2,1,0:T(8,128)(2,1)}, u32[]{:S(2)}) copy-start(bf16[1,128,1792]{2,1,0:T(8,128)(2,1)} %get-tuple-element.24) | copy-start | bytes 1376260

commit v3 on v2

v3 whole, which is shorter than its diff:
```python
import functools

import jax
import jax.numpy as jnp
from jax import lax
from jax.experimental import pallas as pl
from jax.experimental.pallas import tpu as pltpu
from jax.sharding import PartitionSpec as P

F32 = jnp.float32
BF16 = jnp.bfloat16
MESH = pl.DeviceIdType.MESH
SLOTS = 128
RING = 4
LANES = 128
FIRST, MIDDLE, LATE = (0, 64), (64, 96), (96, 128)
EARLY = (0, 96)


HOP = 5


def plan(zs):
    far, near = zs // 2, -(zs - 1 - zs // 2)
    stops = [0]
    for j in range(1, far // HOP + 1):
        stops += [d for d in (HOP * j, -HOP * j) if near <= d <= far]
    seen = set(stops)
    serves = {}
    for stop in stops:
        serves[stop] = []
        for step in range(1, HOP // 2 + 1):
            for off in (step, -step):
                d = stop + off
                if near <= d <= far and d not in seen:
                    seen.add(d)
                    serves[stop].append(off)
    assert len(seen) == zs
    return stops, serves


def dot(left, right, contract=(1, 0)):
    dims = (((contract[0],), (contract[1],)), ((), ()))
    return lax.dot_general(left, right, dims, preferred_element_type=F32)


def kernel(
    sizes,
    tok_ref,
    dy_ref,
    picks_ref,
    gates_ref,
    wg_hbm,
    wu_hbm,
    wd_hbm,
    in_grad_ref,
    gate_grad_ref,
    gg_ref,
    gu_ref,
    gd_ref,
    own_chunk,
    packs,
    ring,
    meta_tok,
    sel_tok,
    gate_slot,
    xd,
    wgu,
    wdn,
    part,
    part_in,
    hid,
    half_out,
    half_in,
    acc,
    acc_out,
    acc_in,
    own_gate,
    gate_rows,
    dense,
    dense_out,
    near_in,
    far_in,
    last_in,
    send_sem,
    recv_sem,
    local_sem,
):
    zs, top = sizes
    toks = 8 * zs
    half = own_chunk.shape[1] - LANES
    colw = 2 * half
    z = lax.axis_index("dp")
    n = lax.axis_index("node")
    x = lax.axis_index("local")
    y = n // 2
    c = n % 2
    stops, serves = plan(zs)
    n_first, n_early = zs // 2, 3 * zs // 4
    order = sorted(range(zs // 2 + 1 - zs, zs // 2 + 1), key=lambda d: (abs(d), -d))
    at = order.index

    offsets = sorted({off for stop in stops for off in serves[stop]} | {HOP, -HOP})
    xr, xl, xo = (x + 1) % RING, (x + 3) % RING, (x + 2) % RING
    yr, yl, yo = (y + 1) % RING, (y + 3) % RING, (y + 2) % RING
    nodes = 2 * RING
    sibling = (z, 2 * y + 1 - c, x)
    y_right, y_left = (z, 2 * yr + c, x), (z, 2 * yl + c, x)
    x_right, x_left, x_over = (z, n, xr), (z, n, xl), (z, n, xo)
    y_over = (z, 2 * yo + c, x)
    moved = x != y

    def across(off):
        return ((z + off + zs) % zs, 2 * x + c, y)

    gate_to = [(z, 2 * x + (c + i % 2) % 2, (x + i // 2) % RING) for i in range(nodes)]
    gate_from = [(z, (n + i) % nodes, y) for i in range(nodes)]

    count = [0]
    sends = []

    def remote(src, dst, device, keep=True):
        i = count[0]
        count[0] += 1
        copy = pltpu.make_async_remote_copy(
            src_ref=src,
            dst_ref=dst,
            send_sem=send_sem.at[i],
            recv_sem=recv_sem.at[i],
            device_id=device,
            device_id_type=MESH,
        )
        if keep:
            sends.append(copy)
        return copy

    row0 = pl.multiple_of(x * colw, LANES)
    loads = [
        pltpu.make_async_copy(
            wg_hbm.at[0, pl.ds(row0, colw), :], wgu.at[:, 0:LANES], local_sem.at[0]
        ),
        pltpu.make_async_copy(
            wu_hbm.at[0, pl.ds(row0, colw), :], wgu.at[:, LANES : 2 * LANES], local_sem.at[1]
        ),
        pltpu.make_async_copy(wd_hbm.at[0, :, pl.ds(row0, colw)], wdn, local_sem.at[2]),
    ]
    for load in loads:
        load.start()

    barrier = pltpu.get_barrier_semaphore()
    peers = [((z + off + zs) % zs, n, x) for off in offsets]
    peers += [(z, n, (x + i) % RING) for i in range(1, RING)]
    peers += [y_right, y_left, y_over, sibling] + gate_from[1:]
    peers += [across(off) for off in offsets]
    for peer in peers:
        pl.semaphore_signal(barrier, inc=1, device_id=peer, device_id_type=MESH)

    @pl.when(moved)
    def _():
        for peer in (across(0), gate_from[0]):
            pl.semaphore_signal(barrier, inc=1, device_id=peer, device_id_type=MESH)

    col0 = pl.multiple_of(y * colw + c * half, LANES)
    own_chunk[:, 0:half] = jnp.concatenate(
        [tok_ref[:, pl.ds(col0, half)].astype(F32), dy_ref[:, pl.ds(col0, half)].astype(F32)],
        axis=0,
    ).astype(BF16)
    place = lax.broadcasted_iota(jnp.int32, (top, LANES), 0)
    lane_k = lax.broadcasted_iota(jnp.int32, (top, LANES), 1)
    put_picks = (lane_k == place).astype(F32).astype(BF16)
    put_gates = (lane_k == 8 + place).astype(F32).astype(BF16)
    meta = dot(picks_ref[...].astype(F32).astype(BF16), put_picks) + dot(gates_ref[...], put_gates)
    own_chunk[:, half:] = jnp.concatenate([meta, meta], axis=0).astype(BF16)

    pl.semaphore_wait(barrier, len(peers) + jnp.where(moved, 2, 0))

    coming = {}
    cross = remote(own_chunk, ring.at[at(0)], across(0), keep=False)

    def pass_on(d, off):
        if d == 0:
            copy = remote(own_chunk, ring.at[at(off)], across(off))
        else:
            copy = remote(ring.at[at(d)], ring.at[at(d + off)], ((z + off + zs) % zs, n, x))
        copy.start()
        coming[d + off] = copy

    def start_cross():
        @pl.when(moved)
        def _():
            cross.start()

        @pl.when(jnp.logical_not(moved))
        def _():
            ring[at(0)] = own_chunk[...]

    for stop in stops:
        if stop != 0:
            coming[stop].wait_recv()
        for step in (HOP, -HOP):
            if stop * step >= 0 and stop + step in stops:
                pass_on(stop, step)
        for off in serves[stop]:
            pass_on(stop, off)
        if stop == 0:
            start_cross()

    @pl.when(moved)
    def _():
        cross.wait_recv()

    expert = z.astype(F32)

    def counts(shape, axis):
        return lax.broadcasted_iota(jnp.int32, shape, axis)

    def named(metas):
        return jnp.logical_and(metas == expert, counts(metas.shape, 1) < top)

    def select(metas, first):
        tall = metas.shape[0]
        t_row, t_col = counts((tall, tall), 0), counts((tall, tall), 1)
        before = jnp.logical_and(t_row // 8 == t_col // 8, t_col < t_row).astype(F32).astype(BF16)
        lane = counts(metas.shape, 1)
        chunk = first + counts(metas.shape, 0) // 8
        home = jnp.where(chunk < n_first, chunk, chunk - n_first + MIDDLE[0] // 4)
        home = jnp.where(chunk < n_early, home, chunk - n_early + LATE[0] // 4)
        chosen = jnp.sum(named(metas).astype(F32), axis=1, keepdims=True)
        chosen = jnp.broadcast_to(chosen, metas.shape)
        rank = dot(before, chosen.astype(BF16))
        ok = jnp.logical_and(chosen > 0.5, rank == (lane % 4).astype(F32))
        return jnp.logical_and(ok, home == lane // 4).astype(F32)

    def pieces(batch):
        rows = slice(*batch)

        def move(p, group, device):
            ref = xd.at[c, p, group, rows]
            return remote(ref, ref, device)

        copies = dict(
            right=[move(p, y, y_right) for p in range(2)],
            left=[move(p, y, y_left) for p in range(2)],
            core=[move(p, y, sibling) for p in range(2)],
            core_l=[move(p, yl, sibling) for p in range(2)],
            core_r=[move(p, yr, sibling) for p in range(2)],
            core_o=[move(p, yo, sibling) for p in range(2)],
        )
        if batch == LATE:
            copies["over"] = [move(p, y, y_over) for p in range(2)]
        else:
            copies["on_right"] = move(0, yl, y_right)
            copies["on_left"] = move(1, yr, y_left)
        return copies

    def send_picked(batch, first, last):
        number = last - first
        for d in coming:
            if d not in stops and first <= at(d) < last:
                coming[d].wait_recv()
        metas = ring[first:last, :, half:].astype(F32)[:, 0:8, :].reshape(8 * number, LANES)
        meta_tok[y, 8 * first : 8 * last] = metas
        cube = select(metas, first).reshape(number, 8, SLOTS)
        blank = jnp.zeros_like(cube)
        pick_rows = jnp.concatenate(
            [jnp.concatenate([cube, blank], axis=2), jnp.concatenate([blank, cube], axis=2)],
            axis=1,
        ).reshape(16 * number, 2 * SLOTS)
        chunks = ring[first:last, :, 0:half].reshape(16 * number, half)
        picked = dot(pick_rows.astype(BF16), chunks, (0, 0)).astype(BF16)
        lo, hi = batch
        xd[c, 0, y, lo:hi] = picked[lo:hi]
        xd[c, 1, y, lo:hi] = picked[SLOTS + lo : SLOTS + hi]
        copies = pieces(batch)
        for copy in copies.get("over", []):
            copy.start()
        copies["right"][0].start()
        copies["left"][1].start()
        copies["right"][1].start()
        copies["left"][0].start()
        copies["core"][0].start()
        copies["core"][1].start()
        return copies

    def relay_picked(copies):
        for p in range(2):
            copies["right"][p].wait_recv()
            if p == 0 and "on_right" in copies:
                copies["on_right"].start()
            copies["core_l"][p].start()
            copies["left"][1 - p].wait_recv()
            if p == 0 and "on_left" in copies:
                copies["on_left"].start()
            copies["core_r"][1 - p].start()

    def finish_picked(copies):
        far = copies["over"] if "over" in copies else [copies["on_right"], copies["on_left"]]
        for p in range(2):
            far[p].wait_recv()
            copies["core_o"][p].start()

    def end_picked(copies):
        for name in ("core", "core_l", "core_r", "core_o"):
            for copy in copies[name]:
                copy.wait_recv()

    early = send_picked(FIRST, 0, n_first)
    middle = send_picked(MIDDLE, n_first, n_early)
    relay_picked(early)
    late = send_picked(LATE, n_early, zs)

    tall = packs.shape[1]
    mine = meta_tok[y]
    if 8 * tall > toks:
        mine = jnp.concatenate([mine, jnp.zeros((8 * tall - toks, LANES), F32)], axis=0)
    packed = mine[0:tall]
    for i in range(1, 8):
        packed = packed + pltpu.roll(mine[i * tall : (i + 1) * tall], 16 * i, 1)
    packs[y] = packed.astype(BF16)
    packs_out = [remote(packs.at[y], packs.at[y], peer) for peer in (y_over, y_right, y_left)]
    for copy in packs_out:
        copy.start()
    relay_picked(middle)
    finish_picked(early)
    relay_picked(late)

    sel_tok[...] = select(meta_tok[y], 0).astype(BF16)
    for copy in packs_out:
        copy.wait_recv()
    for group in range(RING):
        pack = packs[group].astype(F32)
        metas = jnp.concatenate(
            [pack] + [pltpu.roll(pack, LANES - 16 * i, 1) for i in range(1, 8)], axis=0
        )[0:toks]
        chosen = select(metas, 0).astype(BF16)
        gate_of = jnp.where(named(metas), pltpu.roll(metas, LANES - 8, 1), 0.0)
        gate_of = jnp.sum(gate_of, axis=1, keepdims=True)
        gate_of = jnp.broadcast_to(gate_of, (toks, LANES)).astype(BF16)
        gate_slot[group] = dot(chosen, gate_of, (0, 0))

    for load in loads:
        load.wait()
    finish_picked(middle)
    end_picked(early)
    end_picked(middle)

    n_slots = RING * SLOTS

    def halves(batch):
        first, last = batch
        middle = (first + last) // 2
        return slice(first, middle), slice(middle, last)

    def scatter_copies(batch, src, into, r, l, o, right, left, over):
        if batch == LATE:
            rows = slice(*batch)
            return dict(
                far=remote(src.at[o, rows], into.at[0, rows], over),
                right=remote(src.at[r, rows], into.at[1, rows], right),
                left=remote(src.at[l, rows], into.at[2, rows], left),
            )
        lo, hi = halves(batch)
        return dict(
            a1=remote(src.at[o, lo], into.at[0, lo], right),
            b1=remote(src.at[o, hi], into.at[0, hi], left),
            a2=remote(src.at[r, hi], into.at[1, hi], right),
            b2=remote(src.at[l, lo], into.at[2, lo], left),
            a3=remote(src.at[r, lo], into.at[1, lo], right),
            b3=remote(src.at[l, hi], into.at[2, hi], left),
        )

    def send_partial(batch):
        first, last = batch
        tall = RING * (last - first)

        def take(side, p):
            return xd[side, p, :, first:last, :].reshape(tall, half)

        gate_up = dot(take(0, 0), wgu[0:half]) + dot(take(1, 0), wgu[half:])
        back_part = dot(take(0, 1), wdn[:, 0:half], (1, 1)) + dot(
            take(1, 1), wdn[:, half:], (1, 1)
        )
        part[:, first:last, 0:256] = gate_up.reshape(RING, last - first, 256)
        part[:, first:last, 256:] = back_part.reshape(RING, last - first, LANES)
        copies = scatter_copies(batch, part, part_in, xr, xl, xo, x_right, x_left, x_over)
        for name in ("far", "right", "left") if batch == LATE else ("a1", "b1", "a2", "b2"):
            copies[name].start()
        return copies

    def relay_partial(copies, batch):
        lo, hi = halves(batch)
        copies["a1"].wait_recv()
        part[xr, lo] = part[xr, lo] + part_in[0, lo]
        copies["a3"].start()
        copies["b1"].wait_recv()
        part[xl, hi] = part[xl, hi] + part_in[0, hi]
        copies["b3"].start()

    def send_hidden(copies, batch):
        rows = slice(*batch)
        for name in ("far", "right", "left") if batch == LATE else ("a2", "b2", "a3", "b3"):
            copies[name].wait_recv()
        summed = part[x, rows] + part_in[1, rows] + part_in[2, rows]
        if batch == LATE:
            summed = summed + part_in[0, rows]
        gate_pre = summed[:, 0:128]
        up_pre = summed[:, 128:256]
        back = summed[:, 256:384]
        gate_col = gate_slot[x, rows]
        sig = jax.nn.sigmoid(gate_pre)
        act = gate_pre * sig * up_pre
        d_act = gate_col * back
        d_up = d_act * gate_pre * sig
        d_pre = d_act * up_pre * sig * (1.0 + gate_pre * (1.0 - sig))
        hid[x, rows, 0:128] = d_pre.astype(BF16)
        hid[x, rows, 128:256] = d_up.astype(BF16)
        hid[x, rows, 256:384] = act.astype(BF16)
        mine = hid.at[x, rows]
        moves = [remote(mine, mine, x_right), remote(mine, mine, x_left)]
        if batch == LATE:
            moves.append(remote(mine, mine, x_over))
        for move in moves:
            move.start()
        if batch != LATE:
            lo, hi = halves(batch)
            moves.append(remote(hid.at[xl, lo], hid.at[xl, lo], x_right))
            moves.append(remote(hid.at[xr, hi], hid.at[xr, hi], x_left))
        return moves, back * act

    def relay_hidden(moves):
        moves[0].wait_recv()
        moves[2].start()
        moves[1].wait_recv()
        moves[3].start()

    px_early = send_partial(EARLY)
    finish_picked(late)
    relay_partial(px_early, EARLY)
    end_picked(late)
    px_late = send_partial(LATE)
    h_early, gates_early = send_hidden(px_early, EARLY)
    relay_hidden(h_early)
    h_late, gates_late = send_hidden(px_late, LATE)

    gate_parts = jnp.concatenate([gates_early, gates_late], axis=0)
    gate_row = jnp.sum(jnp.transpose(gate_parts), axis=0, keepdims=True)
    own_gate[...] = jnp.broadcast_to(gate_row, (8, SLOTS))
    first_gate = count[0]
    count[0] += nodes

    def gate_copy(i, sender):
        return pltpu.make_async_remote_copy(
            src_ref=own_gate,
            dst_ref=gate_rows.at[sender],
            send_sem=send_sem.at[first_gate + i],
            recv_sem=recv_sem.at[first_gate + sender],
            device_id=gate_to[i],
            device_id_type=MESH,
        )

    gate_out = [gate_copy(i, n) for i in range(nodes)]

    @pl.when(moved)
    def _():
        gate_out[0].start()

    @pl.when(jnp.logical_not(moved))
    def _():
        gate_rows[n] = own_gate[...]

    for copy in gate_out[1:]:
        copy.start()

    for copy in h_early[2:] + h_late:
        copy.wait_recv()

    grads = hid[:, :, 0:256].reshape(n_slots, 256)
    other = pl.multiple_of((1 - c) * half, LANES)
    ours = pl.multiple_of(c * half, LANES)
    half_out[...] = (
        dot(grads, wgu[pl.ds(other, half), :], (1, 1)).astype(BF16).reshape(RING, SLOTS, half)
    )
    core_half = {}
    for batch in (LATE, EARLY):
        rows = slice(*batch)
        core_half[batch] = remote(half_out.at[:, rows], half_in.at[:, rows], sibling)
        core_half[batch].start()
    acc[...] = dot(grads, wgu[pl.ds(ours, half), :], (1, 1)).reshape(RING, SLOTS, half)

    py = {}
    for batch in (LATE, EARLY):
        rows = slice(*batch)
        lo, hi = halves(batch)
        core_half[batch].wait_recv()
        acc[:, rows] = acc[:, rows] + half_in[:, rows].astype(F32)
        py[batch] = scatter_copies(batch, acc_out, acc_in, yr, yl, yo, y_right, y_left, y_over)
        acc_out[yo, rows] = acc[yo, rows].astype(BF16)
        if batch == LATE:
            py[batch]["far"].start()
            acc_out[yr, rows] = acc[yr, rows].astype(BF16)
            py[batch]["right"].start()
            acc_out[yl, rows] = acc[yl, rows].astype(BF16)
            py[batch]["left"].start()
        else:
            py[batch]["a1"].start()
            py[batch]["b1"].start()
            acc_out[yr, hi] = acc[yr, hi].astype(BF16)
            py[batch]["a2"].start()
            acc_out[yl, lo] = acc[yl, lo].astype(BF16)
            py[batch]["b2"].start()

    for sender in range(nodes):

        @pl.when(jnp.logical_or(moved, n != sender))
        def _():
            gate_copy(0, sender).wait_recv()

    gate_sum = gate_rows[0]
    for i in range(1, nodes):
        gate_sum = gate_sum + gate_rows[i]
    gate_tok = jnp.sum(sel_tok[...].astype(F32) * gate_sum[0:1], axis=1, keepdims=True)
    hit = named(meta_tok[y])
    gate_hi = gate_tok.astype(BF16).astype(F32)
    gate_tile = jnp.where(hit, gate_hi, 0.0) + pltpu.roll(
        jnp.where(hit, gate_tok - gate_hi, 0.0), LANES // 2, 1
    )

    def relay_sums(batch):
        lo, hi = halves(batch)
        py[batch]["a1"].wait_recv()
        acc_out[yr, lo] = (acc[yr, lo] + acc_in[0, lo].astype(F32)).astype(BF16)
        py[batch]["a3"].start()
        py[batch]["b1"].wait_recv()
        acc_out[yl, hi] = (acc[yl, hi] + acc_in[0, hi].astype(F32)).astype(BF16)
        py[batch]["b3"].start()

    wide = (half + LANES) // 2

    def spread_sums(batch, first, last):
        rows = slice(*batch)
        for name in ("far", "right", "left") if batch == LATE else ("a2", "b2", "a3", "b3"):
            py[batch][name].wait_recv()
        total = acc[y, rows] + acc_in[1, rows].astype(F32) + acc_in[2, rows].astype(F32)
        if batch == LATE:
            total = total + acc_in[0, rows].astype(F32)
        blank = jnp.zeros((SLOTS - (batch[1] - batch[0]), half), F32)
        total = jnp.concatenate([total, blank] if batch == EARLY else [blank, total], axis=0)
        sel = sel_tok[8 * first : 8 * last]
        one = total.astype(BF16)
        rest = total - one.astype(F32)
        two = rest.astype(BF16)
        three = (rest - two.astype(F32)).astype(BF16)
        spread = dot(sel, one) + (dot(sel, two) + dot(sel, three))
        full = jnp.concatenate([spread, gate_tile[8 * first : 8 * last]], axis=1)
        dense[first:last, 0:8, :] = full[:, 0:wide].reshape(last - first, 8, wide)
        dense[first:last, 8:16, :] = full[:, wide:].reshape(last - first, 8, wide)
        dense_out[first:last] = dense[first:last].astype(BF16)

    near = {}

    def send_near(first, last):
        for stop in reversed(stops):
            for off in serves[stop]:
                if first <= at(stop + off) < last:
                    near[stop, off] = remote(
                        dense_out.at[at(stop + off)],
                        near_in.at[len(near)],
                        across(-off) if stop == 0 else ((z - off + zs) % zs, n, x),
                    )
                    near[stop, off].start()

    spread_sums(LATE, n_early, zs)
    send_near(n_early, zs)
    relay_sums(EARLY)
    spread_sums(EARLY, 0, n_early)
    send_near(0, n_early)
    end = remote(dense_out.at[at(0)], last_in, across(0), keep=False)

    @pl.when(moved)
    def _():
        end.start()

    @pl.when(jnp.logical_not(moved))
    def _():
        last_in[...] = dense_out[at(0)]

    slot_of = {key: i for i, key in enumerate(near)}

    tiles = colw // LANES
    def weight_tile(t):
        side = t // (half // LANES)
        left = pl.multiple_of((t % (half // LANES)) * LANES, LANES)
        down = pl.multiple_of(t * LANES, LANES)
        xs = xd[side, 0, :, :, pl.ds(left, LANES)].reshape(n_slots, LANES)
        ds = xd[side, 1, :, :, pl.ds(left, LANES)].astype(F32)
        scaled = (gate_slot[...] * ds).astype(BF16).reshape(n_slots, LANES)
        both = dot(xs, hid[:, :, 0:256].reshape(n_slots, 256), (0, 0)).astype(BF16)
        gg_ref[0, pl.ds(down, LANES), :] = both[:, 0:128]
        gu_ref[0, pl.ds(down, LANES), :] = both[:, 128:256]
        gd_ref[0, :, pl.ds(down, LANES)] = dot(
            hid[:, :, 256:384].reshape(n_slots, LANES), scaled, (0, 0)
        ).astype(BF16)

    def weight_tiles(first, last):
        def one(t, carry):
            weight_tile(t)
            return carry

        lax.fori_loop(first, last, one, 0)

    levels = len(stops) // 2
    share = -(-tiles // (levels + 1))
    weight_tiles(0, min(share, tiles))
    far = {}
    for i, stop in enumerate(reversed(stops)):
        if stop == 0:

            @pl.when(moved)
            def _():
                end.wait_recv()

        value = last_in[...].astype(F32) if stop == 0 else dense[at(stop)]
        for off in serves[stop]:
            near[stop, off].wait_recv()
            value = value + near_in[slot_of[stop, off]].astype(F32)
        for step in (HOP, -HOP):
            if stop * step >= 0 and stop + step in stops:
                far[stop + step].wait_recv()
                value = value + far_in[stops.index(stop + step) - 1].astype(F32)
        if stop == 0:
            final = value
        else:
            dense_out[at(stop)] = value.astype(BF16)
            back_by = HOP if stop > 0 else -HOP
            far[stop] = remote(
                dense_out.at[at(stop)],
                far_in.at[stops.index(stop) - 1],
                across(-back_by) if stop == back_by else ((z - back_by + zs) % zs, n, x),
            )
            far[stop].start()
            if i % 2 == 1:
                done = share * ((i + 1) // 2)
                weight_tiles(min(done, tiles), min(done + share, tiles))
    final = jnp.concatenate([final[0:8], final[8:16]], axis=1)
    gate_both = final[:, half:]
    gate_grad_ref[...] = gate_both + pltpu.roll(gate_both, LANES // 2, 1)
    in_grad_ref[...] = final[:, 0:half].astype(BF16)

    @pl.when(moved)
    def _():
        cross.wait_send()
        end.wait_send()
        gate_out[0].wait_send()

    for copy in gate_out[1:]:
        copy.wait_send()

    for copy in sends:
        copy.wait_send()


def body(tokens, out_grad, picks, gates, w_gate, w_up, w_down):
    zs = lax.axis_size("dp")
    width = tokens.shape[1]
    top = picks.shape[1]
    half = width // (2 * RING)
    colw = 2 * half
    toks = 8 * zs
    wide = (half + LANES) // 2
    stops, _ = plan(zs)
    hbm_spec = pl.BlockSpec(memory_space=pltpu.HBM)
    vmem_spec = pl.BlockSpec(memory_space=pltpu.VMEM)
    in_grad, gate_grad, gg, gu, gd = pl.pallas_call(
        functools.partial(kernel, (zs, top)),
        out_shape=(
            jax.ShapeDtypeStruct((8, half), BF16),
            jax.ShapeDtypeStruct((8, LANES), F32),
            jax.ShapeDtypeStruct((1, colw, LANES), BF16),
            jax.ShapeDtypeStruct((1, colw, LANES), BF16),
            jax.ShapeDtypeStruct((1, LANES, colw), BF16),
        ),
        in_specs=[vmem_spec] * 4 + [hbm_spec] * 3,
        out_specs=(vmem_spec,) * 5,
        scratch_shapes=[
            pltpu.VMEM((16, half + LANES), BF16),
            pltpu.VMEM((RING, -(-zs // 16) * 16, LANES), BF16),
            pltpu.VMEM((zs, 16, half + LANES), BF16),
            pltpu.VMEM((RING, toks, LANES), F32),
            pltpu.VMEM((toks, SLOTS), BF16),
            pltpu.VMEM((RING, SLOTS, LANES), F32),
            pltpu.VMEM((2, 2, RING, SLOTS, half), BF16),
            pltpu.VMEM((colw, 2 * LANES), BF16),
            pltpu.VMEM((LANES, colw), BF16),
            pltpu.VMEM((RING, SLOTS, 3 * LANES), F32),
            pltpu.VMEM((3, SLOTS, 3 * LANES), F32),
            pltpu.VMEM((RING, SLOTS, 3 * LANES), BF16),
            pltpu.VMEM((RING, SLOTS, half), BF16),
            pltpu.VMEM((RING, SLOTS, half), BF16),
            pltpu.VMEM((RING, SLOTS, half), F32),
            pltpu.VMEM((RING, SLOTS, half), BF16),
            pltpu.VMEM((3, SLOTS, half), BF16),
            pltpu.VMEM((8, SLOTS), F32),
            pltpu.VMEM((2 * RING, 8, SLOTS), F32),
            pltpu.VMEM((zs, 16, wide), F32),
            pltpu.VMEM((zs, 16, wide), BF16),
            pltpu.VMEM((zs - len(stops), 16, wide), BF16),
            pltpu.VMEM((len(stops) - 1, 16, wide), BF16),
            pltpu.VMEM((16, wide), BF16),
            pltpu.SemaphoreType.DMA((112 + 2 * zs,)),
            pltpu.SemaphoreType.DMA((112 + 2 * zs,)),
            pltpu.SemaphoreType.DMA((3,)),
        ],
        compiler_params=pltpu.CompilerParams(
            collective_id=0, has_side_effects=True, vmem_limit_bytes=52 * 1024 * 1024
        ),
    )(tokens, out_grad, picks, gates, w_gate, w_up, w_down)
    return in_grad, gate_grad[:, 0:top], gg, gu, gd


def solution(mesh):
    placed = (
        P(("dp", "local"), None),
        P(("dp", "local"), None),
        P(("dp", "local"), None),
        P(("dp", "local"), None),
        P("dp", None, "node"),
        P("dp", None, "node"),
        P("dp", "node", None),
    )
    return jax.shard_map(
        body,
        mesh=mesh,
        in_specs=placed,
        out_specs=(
            P(("dp", "local"), "node"),
            P(("dp", "local"), None),
            P("dp", "local", "node"),
            P("dp", "local", "node"),
            P("dp", "node", "local"),
        ),
        check_vma=False,
    )
```

time: 140 us -> 137 us (0.979)
  Pallas kernels: 131 us -> 128 us
    pallas_call x1, Pallas kernels: 131 us -> 128 us  [body(): pl.pallas_call(functools.partial(kernel, (zs, top)), out_shape=(jax.Shape...]
    unnamed x7 -> x13, local copies, waits for them, and re-layouts: 7.03 us -> 6.65 us
where the time goes in v3:
time: 137 us; the launch traced here: 135 us
  Pallas kernels  128 us (93%)
  local copies, waits for them, and re-layouts  6.65 us (5%)
    pallas_call x1, Pallas kernels, body(): pl.pallas_call(functools.partial(kernel, (zs, top)), out_shape=(jax.Shape...  128 us
    unnamed x13, local copies, waits for them, and re-layouts  6.65 us

profile of v3, /device:TPU:24, one launch (start us, length us, event | category | flops | bytes accessed | tf_op | source)
XLA Modules:
  0.0 135.3 jit_solution(5135353073597923408)
XLA Ops:
  0.6 0.0 copy-start
  0.6 0.9 copy-done
  1.5 0.0 copy-start.1
  1.5 0.9 copy-done.1
  2.4 0.0 copy-start.2
  2.4 0.7 copy-done.2
  3.1 0.0 copy-start.3
  3.1 0.7 copy-done.3
  3.8 128.0 %shard_map.110 = (bf16[8,896]{1,0:T(8,128)(2,1)S(1)}, f32[8,128]{1,0:T(8,128)S(1)}, bf16[1,1792,128]{2,1,0:T(8,128)(2,1)S(1)}, bf16[1,1792,128]{2,1,0:T(8,128)(2,1)S(1)}, bf16[1,128,1792]{2,1,0:T(8,128)(2,1)S(1)}) custom-call(bf16[8,7168]{1,0:T(8,128)(2,1)S(1)} %copy-done, bf16[8,7168]{1,0:T(8,128)(2,1)S(1)} %copy-done.1, s32[8,8]{1,0:T(8,128)S(1)} %copy-done.2, ...), custom_call_target="tpu_custom_call" | custom-call | tf_op jit(solution)/shard_map/pallas_call | solution.py:673
  131.8 0.6 copy.17
  132.4 0.6 copy.18
  133.0 0.8 copy.19
  133.8 0.8 copy.20
  134.6 0.8 copy.21
Async XLA Ops:
  0.6 0.9 copy-start
  1.5 0.9 copy-start.1
  2.4 0.7 copy-start.2
  3.1 0.7 copy-start.3

commit v4 on v3

--- a/solution.py
+++ b/solution.py
@@ -59,7 +59,9 @@
     gu_ref,
     gd_ref,
     own_chunk,
-    packs,
+    got_chunk,
+    own_meta,
+    got_meta,
     ring,
     meta_tok,
     sel_tok,
@@ -75,12 +77,12 @@
     acc,
     acc_out,
     acc_in,
-    own_gate,
     gate_rows,
     dense,
     dense_out,
     near_in,
     far_in,
+    last_out,
     last_in,
     send_sem,
     recv_sem,
@@ -88,7 +90,7 @@
 ):
     zs, top = sizes
     toks = 8 * zs
-    half = own_chunk.shape[1] - LANES
+    half = own_chunk.shape[1]
     colw = 2 * half
     z = lax.axis_index("dp")
     n = lax.axis_index("node")
@@ -108,13 +110,8 @@
     y_right, y_left = (z, 2 * yr + c, x), (z, 2 * yl + c, x)
     x_right, x_left, x_over = (z, n, xr), (z, n, xl), (z, n, xo)
     y_over = (z, 2 * yo + c, x)
+    across = (z, 2 * x + c, y)
     moved = x != y
-
-    def across(off):
-        return ((z + off + zs) % zs, 2 * x + c, y)
-
-    gate_to = [(z, 2 * x + (c + i % 2) % 2, (x + i // 2) % RING) for i in range(nodes)]
-    gate_from = [(z, (n + i) % nodes, y) for i in range(nodes)]
 
     count = [0]
     sends = []
@@ -150,51 +147,65 @@
     barrier = pltpu.get_barrier_semaphore()
     peers = [((z + off + zs) % zs, n, x) for off in offsets]
     peers += [(z, n, (x + i) % RING) for i in range(1, RING)]
-    peers += [y_right, y_left, y_over, sibling] + gate_from[1:]
-    peers += [across(off) for off in offsets]
+    peers += [(z, (n + i) % nodes, x) for i in range(1, nodes)]
     for peer in peers:
         pl.semaphore_signal(barrier, inc=1, device_id=peer, device_id_type=MESH)
 
     @pl.when(moved)
     def _():
-        for peer in (across(0), gate_from[0]):
-            pl.semaphore_signal(barrier, inc=1, device_id=peer, device_id_type=MESH)
+        pl.semaphore_signal(barrier, inc=1, device_id=across, device_id_type=MESH)
 
     col0 = pl.multiple_of(y * colw + c * half, LANES)
-    own_chunk[:, 0:half] = jnp.concatenate(
+    own_chunk[...] = jnp.concatenate(
         [tok_ref[:, pl.ds(col0, half)].astype(F32), dy_ref[:, pl.ds(col0, half)].astype(F32)],
         axis=0,
     ).astype(BF16)
     place = lax.broadcasted_iota(jnp.int32, (top, LANES), 0)
     lane_k = lax.broadcasted_iota(jnp.int32, (top, LANES), 1)
-    put_picks = (lane_k == place).astype(F32).astype(BF16)
-    put_gates = (lane_k == 8 + place).astype(F32).astype(BF16)
+    put_picks = (lane_k == 32 * x + place).astype(F32).astype(BF16)
+    put_gates = (lane_k == 32 * x + 8 + place).astype(F32).astype(BF16)
     meta = dot(picks_ref[...].astype(F32).astype(BF16), put_picks) + dot(gates_ref[...], put_gates)
-    own_chunk[:, half:] = jnp.concatenate([meta, meta], axis=0).astype(BF16)
-
-    pl.semaphore_wait(barrier, len(peers) + jnp.where(moved, 2, 0))
+    own_meta[...] = jnp.concatenate([meta, meta], axis=0).astype(BF16)
+    got_meta[x] = own_meta[...]
+
+    pl.semaphore_wait(barrier, len(peers) + jnp.where(moved, 1, 0))
+
+    cross = remote(own_chunk, got_chunk, across, keep=False)
+
+    @pl.when(moved)
+    def _():
+        cross.start()
+
+    @pl.when(jnp.logical_not(moved))
+    def _():
+        got_chunk[...] = own_chunk[...]
+
+    metas = [
+        remote(own_meta, got_meta.at[x], (z, n, (x + i) % RING)) for i in range(1, RING)
+    ]
+    for copy in metas:
+        copy.start()
+    for copy in metas:
+        copy.wait_recv()
+    ring[at(0), :, half:] = (
+        (got_meta[0].astype(F32) + got_meta[1].astype(F32))
+        + (got_meta[2].astype(F32) + got_meta[3].astype(F32))
+    ).astype(BF16)
+
+    @pl.when(moved)
+    def _():
+        cross.wait_recv()
+
+    ring[at(0), :, 0:half] = got_chunk[...]
 
     coming = {}
-    cross = remote(own_chunk, ring.at[at(0)], across(0), keep=False)
 
     def pass_on(d, off):
-        if d == 0:
-            copy = remote(own_chunk, ring.at[at(off)], across(off))
-        else:
-            copy = remote(ring.at[at(d)], ring.at[at(d + off)], ((z + off + zs) % zs, n, x))
+        copy = remote(ring.at[at(d)], ring.at[at(d + off)], ((z + off + zs) % zs, n, x))
         copy.start()
         coming[d + off] = copy
 
-    def start_cross():
-        @pl.when(moved)
-        def _():
-            cross.start()
-
-        @pl.when(jnp.logical_not(moved))
-        def _():
-            ring[at(0)] = own_chunk[...]
-
-    for stop in stops:
+    def serve(stop):
         if stop != 0:
             coming[stop].wait_recv()
         for step in (HOP, -HOP):
@@ -202,22 +213,22 @@
                 pass_on(stop, step)
         for off in serves[stop]:
             pass_on(stop, off)
-        if stop == 0:
-            start_cross()
-
-    @pl.when(moved)
-    def _():
-        cross.wait_recv()
+
+    soon = [stop for stop in stops if abs(stop) <= zs // 4 + HOP // 2]
+    for stop in soon:
+        serve(stop)
 
     expert = z.astype(F32)
 
     def counts(shape, axis):
         return lax.broadcasted_iota(jnp.int32, shape, axis)
 
-    def named(metas):
-        return jnp.logical_and(metas == expert, counts(metas.shape, 1) < top)
-
-    def select(metas, first):
+    def named(metas, group):
+        lane = counts(metas.shape, 1)
+        near = jnp.logical_and(lane >= 32 * group, lane < 32 * group + top)
+        return jnp.logical_and(metas == expert, near)
+
+    def select(metas, group, first):
         tall = metas.shape[0]
         t_row, t_col = counts((tall, tall), 0), counts((tall, tall), 1)
         before = jnp.logical_and(t_row // 8 == t_col // 8, t_col < t_row).astype(F32).astype(BF16)
@@ -225,7 +236,7 @@
         chunk = first + counts(metas.shape, 0) // 8
         home = jnp.where(chunk < n_first, chunk, chunk - n_first + MIDDLE[0] // 4)
         home = jnp.where(chunk < n_early, home, chunk - n_early + LATE[0] // 4)
-        chosen = jnp.sum(named(metas).astype(F32), axis=1, keepdims=True)
+        chosen = jnp.sum(named(metas, group).astype(F32), axis=1, keepdims=True)
         chosen = jnp.broadcast_to(chosen, metas.shape)
         rank = dot(before, chosen.astype(BF16))
         ok = jnp.logical_and(chosen > 0.5, rank == (lane % 4).astype(F32))
@@ -255,12 +266,12 @@
 
     def send_picked(batch, first, last):
         number = last - first
-        for d in coming:
+        for d in order:
             if d not in stops and first <= at(d) < last:
                 coming[d].wait_recv()
         metas = ring[first:last, :, half:].astype(F32)[:, 0:8, :].reshape(8 * number, LANES)
-        meta_tok[y, 8 * first : 8 * last] = metas
-        cube = select(metas, first).reshape(number, 8, SLOTS)
+        meta_tok[8 * first : 8 * last] = metas
+        cube = select(metas, y, first).reshape(number, 8, SLOTS)
         blank = jnp.zeros_like(cube)
         pick_rows = jnp.concatenate(
             [jnp.concatenate([cube, blank], axis=2), jnp.concatenate([blank, cube], axis=2)],
@@ -305,41 +316,26 @@
                 copy.wait_recv()
 
     early = send_picked(FIRST, 0, n_first)
+    for stop in stops[len(soon) :]:
+        serve(stop)
     middle = send_picked(MIDDLE, n_first, n_early)
-    relay_picked(early)
     late = send_picked(LATE, n_early, zs)
 
-    tall = packs.shape[1]
-    mine = meta_tok[y]
-    if 8 * tall > toks:
-        mine = jnp.concatenate([mine, jnp.zeros((8 * tall - toks, LANES), F32)], axis=0)
-    packed = mine[0:tall]
-    for i in range(1, 8):
-        packed = packed + pltpu.roll(mine[i * tall : (i + 1) * tall], 16 * i, 1)
-    packs[y] = packed.astype(BF16)
-    packs_out = [remote(packs.at[y], packs.at[y], peer) for peer in (y_over, y_right, y_left)]
-    for copy in packs_out:
-        copy.start()
-    relay_picked(middle)
-    finish_picked(early)
-    relay_picked(late)
-
-    sel_tok[...] = select(meta_tok[y], 0).astype(BF16)
-    for copy in packs_out:
-        copy.wait_recv()
+    meta_all = meta_tok[...]
+    rolled = pltpu.roll(meta_all, LANES - 8, 1)
     for group in range(RING):
-        pack = packs[group].astype(F32)
-        metas = jnp.concatenate(
-            [pack] + [pltpu.roll(pack, LANES - 16 * i, 1) for i in range(1, 8)], axis=0
-        )[0:toks]
-        chosen = select(metas, 0).astype(BF16)
-        gate_of = jnp.where(named(metas), pltpu.roll(metas, LANES - 8, 1), 0.0)
-        gate_of = jnp.sum(gate_of, axis=1, keepdims=True)
+        chosen = select(meta_all, group, 0).astype(BF16)
+        sel_tok[group] = chosen
+        gate_of = jnp.sum(jnp.where(named(meta_all, group), rolled, 0.0), axis=1, keepdims=True)
         gate_of = jnp.broadcast_to(gate_of, (toks, LANES)).astype(BF16)
         gate_slot[group] = dot(chosen, gate_of, (0, 0))
 
     for load in loads:
         load.wait()
+    relay_picked(early)
+    relay_picked(middle)
+    relay_picked(late)
+    finish_picked(early)
     finish_picked(middle)
     end_picked(early)
     end_picked(middle)
@@ -444,31 +440,11 @@
 
     gate_parts = jnp.concatenate([gates_early, gates_late], axis=0)
     gate_row = jnp.sum(jnp.transpose(gate_parts), axis=0, keepdims=True)
-    own_gate[...] = jnp.broadcast_to(gate_row, (8, SLOTS))
-    first_gate = count[0]
-    count[0] += nodes
-
-    def gate_copy(i, sender):
-        return pltpu.make_async_remote_copy(
-            src_ref=own_gate,
-            dst_ref=gate_rows.at[sender],
-            send_sem=send_sem.at[first_gate + i],
-            recv_sem=recv_sem.at[first_gate + sender],
-            device_id=gate_to[i],
-            device_id_type=MESH,
-        )
-
-    gate_out = [gate_copy(i, n) for i in range(nodes)]
-
-    @pl.when(moved)
-    def _():
-        gate_out[0].start()
-
-    @pl.when(jnp.logical_not(moved))
-    def _():
-        gate_rows[n] = own_gate[...]
-
-    for copy in gate_out[1:]:
+    gate_rows[n] = jnp.broadcast_to(gate_row, (8, SLOTS))
+    rows_out = [
+        remote(gate_rows.at[n], gate_rows.at[n], (z, (n + i) % nodes, x)) for i in range(1, nodes)
+    ]
+    for copy in rows_out:
         copy.start()
 
     for copy in h_early[2:] + h_late:
@@ -509,17 +485,17 @@
             acc_out[yl, lo] = acc[yl, lo].astype(BF16)
             py[batch]["b2"].start()
 
-    for sender in range(nodes):
-
-        @pl.when(jnp.logical_or(moved, n != sender))
-        def _():
-            gate_copy(0, sender).wait_recv()
-
+    for copy in rows_out:
+        copy.wait_recv()
     gate_sum = gate_rows[0]
     for i in range(1, nodes):
         gate_sum = gate_sum + gate_rows[i]
-    gate_tok = jnp.sum(sel_tok[...].astype(F32) * gate_sum[0:1], axis=1, keepdims=True)
-    hit = named(meta_tok[y])
+    gate_tok = jnp.sum(sel_tok[x].astype(F32) * gate_sum[0:1], axis=1, keepdims=True)
+    meta_x = jnp.zeros((toks, LANES), F32)
+    for i in range(RING):
+        turned = meta_tok[...] if i == 0 else pltpu.roll(meta_tok[...], LANES - 32 * i, 1)
+        meta_x = jnp.where(x == i, turned, meta_x)
+    hit = jnp.logical_and(meta_x == expert, counts((toks, LANES), 1) < top)
     gate_hi = gate_tok.astype(BF16).astype(F32)
     gate_tile = jnp.where(hit, gate_hi, 0.0) + pltpu.roll(
         jnp.where(hit, gate_tok - gate_hi, 0.0), LANES // 2, 1
@@ -545,7 +521,7 @@
             total = total + acc_in[0, rows].astype(F32)
         blank = jnp.zeros((SLOTS - (batch[1] - batch[0]), half), F32)
         total = jnp.concatenate([total, blank] if batch == EARLY else [blank, total], axis=0)
-        sel = sel_tok[8 * first : 8 * last]
+        sel = sel_tok[y, 8 * first : 8 * last]
         one = total.astype(BF16)
         rest = total - one.astype(F32)
         two = rest.astype(BF16)
@@ -565,7 +541,7 @@
                     near[stop, off] = remote(
                         dense_out.at[at(stop + off)],
                         near_in.at[len(near)],
-                        across(-off) if stop == 0 else ((z - off + zs) % zs, n, x),
+                        ((z - off + zs) % zs, n, x),
                     )
                     near[stop, off].start()
 
@@ -574,16 +550,6 @@
     relay_sums(EARLY)
     spread_sums(EARLY, 0, n_early)
     send_near(0, n_early)
-    end = remote(dense_out.at[at(0)], last_in, across(0), keep=False)
-
-    @pl.when(moved)
-    def _():
-        end.start()
-
-    @pl.when(jnp.logical_not(moved))
-    def _():
-        last_in[...] = dense_out[at(0)]
-
     slot_of = {key: i for i, key in enumerate(near)}
 
     tiles = colw // LANES
@@ -613,13 +579,7 @@
     weight_tiles(0, min(share, tiles))
     far = {}
     for i, stop in enumerate(reversed(stops)):
-        if stop == 0:
-
-            @pl.when(moved)
-            def _():
-                end.wait_recv()
-
-        value = last_in[...].astype(F32) if stop == 0 else dense[at(stop)]
+        value = dense[at(stop)]
         for off in serves[stop]:
             near[stop, off].wait_recv()
             value = value + near_in[slot_of[stop, off]].astype(F32)
@@ -635,7 +595,7 @@
             far[stop] = remote(
                 dense_out.at[at(stop)],
                 far_in.at[stops.index(stop) - 1],
-                across(-back_by) if stop == back_by else ((z - back_by + zs) % zs, n, x),
+                ((z - back_by + zs) % zs, n, x),
             )
             far[stop].start()
             if i % 2 == 1:
@@ -644,16 +604,24 @@
     final = jnp.concatenate([final[0:8], final[8:16]], axis=1)
     gate_both = final[:, half:]
     gate_grad_ref[...] = gate_both + pltpu.roll(gate_both, LANES // 2, 1)
-    in_grad_ref[...] = final[:, 0:half].astype(BF16)
+    last_out[...] = final[:, 0:half]
+    end = remote(last_out, last_in, across, keep=False)
+
+    @pl.when(moved)
+    def _():
+        end.start()
+        end.wait_recv()
+
+    @pl.when(jnp.logical_not(moved))
+    def _():
+        last_in[...] = last_out[...]
+
+    in_grad_ref[...] = last_in[...].astype(BF16)
 
     @pl.when(moved)
     def _():
         cross.wait_send()
         end.wait_send()
-        gate_out[0].wait_send()
-
-    for copy in gate_out[1:]:
-        copy.wait_send()
 
     for copy in sends:
         copy.wait_send()
@@ -682,11 +650,13 @@
         in_specs=[vmem_spec] * 4 + [hbm_spec] * 3,
         out_specs=(vmem_spec,) * 5,
         scratch_shapes=[
-            pltpu.VMEM((16, half + LANES), BF16),
-            pltpu.VMEM((RING, -(-zs // 16) * 16, LANES), BF16),
+            pltpu.VMEM((16, half), BF16),
+            pltpu.VMEM((16, half), BF16),
+            pltpu.VMEM((16, LANES), BF16),
+            pltpu.VMEM((RING, 16, LANES), BF16),
             pltpu.VMEM((zs, 16, half + LANES), BF16),
-            pltpu.VMEM((RING, toks, LANES), F32),
-            pltpu.VMEM((toks, SLOTS), BF16),
+            pltpu.VMEM((toks, LANES), F32),
+            pltpu.VMEM((RING, toks, SLOTS), BF16),
             pltpu.VMEM((RING, SLOTS, LANES), F32),
             pltpu.VMEM((2, 2, RING, SLOTS, half), BF16),
             pltpu.VMEM((colw, 2 * LANES), BF16),
@@ -699,13 +669,13 @@
             pltpu.VMEM((RING, SLOTS, half), F32),
             pltpu.VMEM((RING, SLOTS, half), BF16),
             pltpu.VMEM((3, SLOTS, half), BF16),
-            pltpu.VMEM((8, SLOTS), F32),
             pltpu.VMEM((2 * RING, 8, SLOTS), F32),
             pltpu.VMEM((zs, 16, wide), F32),
             pltpu.VMEM((zs, 16, wide), BF16),
             pltpu.VMEM((zs - len(stops), 16, wide), BF16),
             pltpu.VMEM((len(stops) - 1, 16, wide), BF16),
-            pltpu.VMEM((16, wide), BF16),
+            pltpu.VMEM((8, half), F32),
+            pltpu.VMEM((8, half), F32),
             pltpu.SemaphoreType.DMA((112 + 2 * zs,)),
             pltpu.SemaphoreType.DMA((112 + 2 * zs,)),
             pltpu.SemaphoreType.DMA((3,)),

time: 137 us -> 133 us (0.971)
  Pallas kernels: 128 us -> 123 us
    pallas_call x1, Pallas kernels: 128 us -> 123 us  [body(): pl.pallas_call(functools.partial(kernel, (zs, top)), out_shape=(jax.Shape...]
where the time goes in v4:
time: 133 us; the launch traced here: 131 us
  Pallas kernels  123 us (92%)
  local copies, waits for them, and re-layouts  6.65 us (5%)
    pallas_call x1, Pallas kernels, body(): pl.pallas_call(functools.partial(kernel, (zs, top)), out_shape=(jax.Shape...  123 us
    unnamed x13, local copies, waits for them, and re-layouts  6.65 us

profile of v4, /device:TPU:24, one launch (start us, length us, event | category | flops | bytes accessed | tf_op | source)
XLA Modules:
  0.0 130.7 jit_solution(7575704023579966965)
XLA Ops:
  0.6 0.0 copy-start
  0.6 0.9 copy-done
  1.5 0.0 copy-start.1
  1.5 0.9 copy-done.1
  2.4 0.0 copy-start.2
  2.4 0.7 copy-done.2
  3.1 0.0 copy-start.3
  3.1 0.7 copy-done.3
  3.8 123.4 %shard_map.110 = (bf16[8,896]{1,0:T(8,128)(2,1)S(1)}, f32[8,128]{1,0:T(8,128)S(1)}, bf16[1,1792,128]{2,1,0:T(8,128)(2,1)S(1)}, bf16[1,1792,128]{2,1,0:T(8,128)(2,1)S(1)}, bf16[1,128,1792]{2,1,0:T(8,128)(2,1)S(1)}) custom-call(bf16[8,7168]{1,0:T(8,128)(2,1)S(1)} %copy-done, bf16[8,7168]{1,0:T(8,128)(2,1)S(1)} %copy-done.1, s32[8,8]{1,0:T(8,128)S(1)} %copy-done.2, ...), custom_call_target="tpu_custom_call" | custom-call | tf_op jit(solution)/shard_map/pallas_call | solution.py:641
  127.2 0.6 copy.17
  127.8 0.6 copy.18
  128.4 0.8 copy.19
  129.2 0.8 copy.20
  129.9 0.8 copy.21
Async XLA Ops:
  0.6 0.9 copy-start
  1.5 0.9 copy-start.1
  2.4 0.7 copy-start.2
  3.1 0.7 copy-start.3

commit v5 on v4

--- a/solution.py
+++ b/solution.py
@@ -576,7 +576,8 @@
 
     levels = len(stops) // 2
     share = -(-tiles // (levels + 1))
-    weight_tiles(0, min(share, tiles))
+    lead = max(0, tiles - levels * share)
+    weight_tiles(0, lead)
     far = {}
     for i, stop in enumerate(reversed(stops)):
         value = dense[at(stop)]
@@ -599,7 +600,7 @@
             )
             far[stop].start()
             if i % 2 == 1:
-                done = share * ((i + 1) // 2)
+                done = lead + share * ((i - 1) // 2)
                 weight_tiles(min(done, tiles), min(done + share, tiles))
     final = jnp.concatenate([final[0:8], final[8:16]], axis=1)
     gate_both = final[:, half:]

time: 133 us -> 133 us (level)
  no operation moved by 1% of the time
where the time goes in v5:
time: 133 us; the launch traced here: 131 us
  Pallas kernels  123 us (92%)
  local copies, waits for them, and re-layouts  6.65 us (5%)
    pallas_call x1, Pallas kernels, body(): pl.pallas_call(functools.partial(kernel, (zs, top)), out_shape=(jax.Shape...  123 us
    unnamed x13, local copies, waits for them, and re-layouts  6.65 us

profile of v5, /device:TPU:24, one launch (start us, length us, event | category | flops | bytes accessed | tf_op | source)
XLA Modules:
  0.0 130.7 jit_solution(3947470057113394905)
XLA Ops:
  0.6 0.0 copy-start
  0.6 0.9 copy-done
  1.5 0.0 copy-start.1
  1.5 0.9 copy-done.1
  2.4 0.0 copy-start.2
  2.4 0.7 copy-done.2
  3.1 0.0 copy-start.3
  3.1 0.7 copy-done.3
  3.8 123.4 %shard_map.110 = (bf16[8,896]{1,0:T(8,128)(2,1)S(1)}, f32[8,128]{1,0:T(8,128)S(1)}, bf16[1,1792,128]{2,1,0:T(8,128)(2,1)S(1)}, bf16[1,1792,128]{2,1,0:T(8,128)(2,1)S(1)}, bf16[1,128,1792]{2,1,0:T(8,128)(2,1)S(1)}) custom-call(bf16[8,7168]{1,0:T(8,128)(2,1)S(1)} %copy-done, bf16[8,7168]{1,0:T(8,128)(2,1)S(1)} %copy-done.1, s32[8,8]{1,0:T(8,128)S(1)} %copy-done.2, ...), custom_call_target="tpu_custom_call" | custom-call | tf_op jit(solution)/shard_map/pallas_call | solution.py:642
  127.2 0.6 copy.17
  127.8 0.6 copy.18
  128.4 0.8 copy.19
  129.2 0.8 copy.20
  129.9 0.8 copy.21
Async XLA Ops:
  0.6 0.9 copy-start
  1.5 0.9 copy-start.1
  2.4 0.7 copy-start.2
  3.1 0.7 copy-start.3
